TPU v7x, 768 devices: a whole 4x8x12 slice. The times are simulated.
768 devices in a mesh: dom: 24 (over z, core), feat: 32 (over y, x).
Axes of the slice: x: 4, y: 8, z: 12, core: 2. Of those that a mesh axis runs over, the one named last changes fastest.
Arguments:
- features: bfloat16 [512, 24576], P('feat', 'dom'), may hold values from -6 to 6
- self_weight: bfloat16 [512, 512], P(None, 'feat'), may hold values from -0.25 to 0.25
- neigh_weight: bfloat16 [512, 512], P(None, 'feat'), may hold values from -0.25 to 0.25
- cotangent: bfloat16 [512, 24576], P('feat', 'dom'), may hold values from -6 to 6
- neighbours: int32 [24576, 16], P('dom'), may hold values from 0 to 1279
- degrees: int32 [24576], P('dom'), may hold values from 1 to 16
- send_rows: int32 [48, 128], P('dom'), may hold values from 0 to 1023
- send_count: int32 [48], P('dom'), may hold values from 32 to 128, as said below
Outputs:
- activated: bfloat16 [512, 24576], P('feat', 'dom')
- grad_x: float32 [512, 24576], P('feat', 'dom')
- grad_self: float32 [512, 512], P(None, 'feat')
- grad_neigh: float32 [512, 512], P(None, 'feat')
Inputs may be any that keep to these rules, and one draw needn't show every extreme that they name: `neighbours`: indices into the extended rows of the node's partition: its 1024 own nodes, then the 128 slots from the partition before it, then the 128 from the one after. `send_rows`: local node indices within the sending partition. `send_count`: some list is full.
All inputs are finite; a program needn't handle non-finite values.
Results may differ from a plain program's by a relative error of at most 0.0046.
Values may be sent and summed in bfloat16 or wider, within the bound.
A program may use at most 32 MiB of HBM per device.

v0:
```python
import math

import jax
import jax.numpy as jnp
from jax import lax
from jax.sharding import PartitionSpec as P


def extended_2(block, sides, width):
    for axis, dim in sides:
        count = lax.axis_size(axis)
        forward = [(i, i + 1) for i in range(count - 1)]
        forward.append((count - 1, 0))
        backward = [(target, source) for source, target in forward]
        low = lax.ppermute(
            lax.slice_in_dim(block, block.shape[dim] - width, None, axis=dim), axis, forward
        )
        high = lax.ppermute(lax.slice_in_dim(block, 0, width, axis=dim), axis, backward)
        block = jnp.concatenate([low, block, high], axis=dim)
    return block


def edge_weights(degrees, slots):
    counted = jnp.arange(slots, dtype=jnp.int32)[:, None] < degrees[None, :]
    return jnp.where(counted, 1.0, 0.0).astype(jnp.float32) / degrees[None, :].astype(jnp.float32)


def gather_sum(extended, neighbour_t, weights):
    picked = extended[:, neighbour_t].astype(jnp.float32)
    return jnp.sum(picked * weights[None], axis=1)


def spread_sum(grad_block, neighbour_t, weights, total_width):
    zeros_grid = jnp.zeros((grad_block.shape[0], total_width), jnp.float32)
    return zeros_grid.at[:, neighbour_t].add(grad_block[:, None, :] * weights[None])


def contract_first(weight_block, columns):
    return lax.dot_general(
        weight_block, columns, (((0,), (0,)), ((), ())), preferred_element_type=jnp.float32
    )


def contract_last(columns, grad_block):
    return lax.dot_general(
        columns, grad_block, (((1,), (1,)), ((), ())), preferred_element_type=jnp.float32
    )


def per_device(
    features, self_weight, neigh_weight, cotangent, neighbours, degrees, send_rows, send_count
):
    local_width, local_nodes = features.shape
    slot_count = send_rows.shape[1]
    neighbour_t = neighbours.T
    weights = edge_weights(degrees, neighbours.shape[1])
    alive_mask = jnp.arange(slot_count, dtype=jnp.int32)[None, :] < send_count[:, None]
    picked = jnp.where(alive_mask[None], features[:, send_rows], jnp.zeros((), features.dtype))
    outgoing = picked.reshape(local_width, 2 * slot_count)
    arrived = extended_2(outgoing, (("dom", 1),), slot_count)
    extended = jnp.concatenate(
        [features, arrived[:, :slot_count], arrived[:, 3 * slot_count :]], axis=1
    )
    aggregate_rows = gather_sum(extended, neighbour_t, weights).astype(jnp.bfloat16)
    full_x, full_agg = (
        lax.all_gather(features, "feat", axis=0, tiled=True),
        lax.all_gather(aggregate_rows, "feat", axis=0, tiled=True),
    )
    preact = contract_first(self_weight, full_x) + contract_first(neigh_weight, full_agg)
    activated = jax.nn.silu(preact).astype(jnp.bfloat16)
    sigmoid_z = jax.nn.sigmoid(preact)
    pre_grad = (
        cotangent.astype(jnp.float32) * sigmoid_z * (1.0 + preact * (1.0 - sigmoid_z))
    ).astype(jnp.bfloat16)
    factor = 1.0 / math.sqrt(local_nodes * lax.axis_size("dom"))
    self_part = contract_last(full_x, pre_grad)
    neigh_part = contract_last(full_agg, pre_grad)
    grad_self, grad_neigh = lax.psum((self_part, neigh_part), "dom")
    summed = lax.psum_scatter(
        jnp.concatenate(
            [
                jnp.dot(self_weight, pre_grad, preferred_element_type=jnp.float32),
                jnp.dot(neigh_weight, pre_grad, preferred_element_type=jnp.float32),
            ],
            axis=1,
        ),
        "feat",
        scatter_dimension=0,
        tiled=True,
    )
    direct_grad = summed[:, :local_nodes]
    agg_grad = summed[:, local_nodes:]
    ext_grad = spread_sum(agg_grad, neighbour_t, weights, local_nodes + 2 * slot_count)
    returned = extended_2(ext_grad[:, local_nodes:], (("dom", 1),), slot_count)
    back_rows = jnp.stack([returned[:, :slot_count], returned[:, 3 * slot_count :]], axis=1)
    back_rows = jnp.where(alive_mask[None], back_rows, 0.0)
    local_grad = (
        ext_grad[:, :local_nodes]
        .at[:, send_rows.reshape(-1)]
        .add(back_rows.reshape(local_width, 2 * slot_count))
    )
    grad_x = direct_grad + local_grad
    return (activated, grad_x, grad_self * factor, grad_neigh * factor)


def solution(mesh):
    return jax.shard_map(
        per_device,
        mesh=mesh,
        in_specs=(
            P("feat", "dom"),
            P(None, "feat"),
            P(None, "feat"),
            P("feat", "dom"),
            P("dom", None),
            P("dom"),
            P("dom", None),
            P("dom"),
        ),
        out_specs=(P("feat", "dom"), P("feat", "dom"), P(None, "feat"), P(None, "feat")),
        check_vma=False,
    )
```

profile of v0, /device:TPU:1, one launch (start us, length us, event | category | flops | bytes accessed | tf_op | source)
XLA Modules:
  0.0 692.3 jit_solution(4118666518562754406)
XLA Ops:
  7.2 0.0 all-gather.3.cloned.1.call-start
  7.2 0.7 all-gather.3.cloned.1.call-update
  7.9 0.0 all-gather.5.cloned.1.call-start
  8.0 0.9 copy.32
  8.9 0.7 lt.63
  9.6 0.7 fusion.5
  10.3 0.9 gather_fusion
  11.2 0.1 copy.39
  11.3 3.5 collective-permute-start
  14.8 7.1 %collective-permute-start.1 = (bf16[16,128]{1,0:T(8,128)(2,1)S(1)}, bf16[16,128]{1,0:T(8,128)(2,1)S(1)}, u32[]{:S(2)}, u32[]{:S(2)}) collective-permute-start(bf16[16,128]{1,0:T(8,128)(2,1)S(1)} %get-tuple-element.29), channel_id=1, source_target_pairs={{32,0},{64,32},{96,64},{128,96},{160,128},{192,160},{224,192},{256... | collective-permute-start | bytes 12296 | tf_op jit(solution)/shard_map/ppermute | solution.py:18
  21.8 0.7 convert_element_type.20
  22.5 0.8 fusion.4
  23.4 0.7 select_divide_fusion
  24.1 0.8 pad_maximum_fusion.2
  24.9 0.2 copy.34
  25.1 57.8 %gather_fusion.1 = bf16[16384,16]{1,0:T(8,128)(2,1)} fusion(bf16[16,1280]{0,1:T(8,128)(2,1)S(1)} %copy.34, s32[16384]{0:T(1024)S(1)} %broadcast_clamp_fusion), kind=kCustom, calls=%fused_computation.1 | custom fusion | bytes 1114112 | tf_op jit(solution)/shard_map/gather | solution.py:29
  83.0 4.5 fusion
  87.4 0.7 copy.35
  88.2 0.0 all-gather.5.cloned.1.call-update
  88.2 0.0 all-reduce.3.cloned.1.call-start
  88.2 13.7 %all-gather.3.cloned.1.call-done = bf16[512,1024]{1,0:T(8,128)(2,1)} async-done(((bf16[16,1024]{1,0:T(8,128)(2,1)}), bf16[512,1024]{1,0:T(8,128)(2,1)}) %all-gather.3.cloned.1.call-update) | async-done | bytes 1048592 | tf_op jit(solution)/shard_map/all_gather | solution.py:66
  101.9 1.6 fusion.9
  103.5 87.8 %all-gather.5.cloned.1.call-done = bf16[512,1024]{1,0:T(8,128)(2,1)} async-done(((bf16[16,1024]{1,0:T(8,128)(2,1)}), bf16[512,1024]{1,0:T(8,128)(2,1)}) %all-gather.5.cloned.1.call-update) | async-done | bytes 1048592 | tf_op jit(solution)/shard_map/all_gather | solution.py:67
  191.2 2.2 multiply_convert_fusion
  193.4 0.5 convolution_bitcast_fusion
  193.9 1.8 convolution_bitcast_fusion.1
  195.7 1.0 fusion.10
  196.7 1.0 convolution_bitcast_fusion.3
  197.7 0.0 reduce-scatter.4.cloned.1.call-start
  197.8 4.0 pad_maximum_fusion
  201.8 5.4 copy.40
  207.2 0.7 copy-done.5
  207.8 141.1 %all-reduce.3.cloned.1.call-done = (f32[512,16]{0,1:T(8,128)}, f32[512,16]{0,1:T(8,128)}) async-done(((f32[512,16]{0,1:T(8,128)}, f32[512,16]{0,1:T(8,128)}), (f32[512,16]{0,1:T(8,128)}, f32[512,16]{0,1:T(8,128)})) %all-reduce.3.cloned.1.call-update) | async-done | bytes 65552 | tf_op jit(solution)/shard_map/psum | solution.py:78
  349.0 1.4 broadcast_multiply_fusion.1
  350.4 228.6 %reduce-scatter.4.cloned.1.call-done = f32[16,2048]{1,0:T(8,128)} async-done(((f32[512,2048]{1,0:T(8,128)}), f32[16,2048]{1,0:T(8,128)}) %reduce-scatter.4.cloned.1.call-update) | async-done | bytes 131088
  579.0 0.9 fusion.7
  579.9 0.2 copy.43
  580.1 0.2 copy.42
  580.3 4.5 broadcast_multiply_fusion
  584.8 87.8 %scatter_custom_fusion = f32[16,1280]{0,1:T(8,128)S(1)} fusion(s32[16384]{0:T(1024)S(1)} %bitcast.58, f32[16384,16]{1,0:T(8,128)} %bitcast.53, f32[]{:T(128)} %constant.12.clone.1), kind=kCustom, calls=%fused_computation.14 | custom fusion | flops 262144 | bytes 82432 | tf_op jit(solution)/shard_map/scatter-add | solution.py:35
  672.6 6.3 collective-permute-start.2
  679.0 0.1 slice_add_fusion
  679.0 1.3 collective-permute-done.2
  680.3 2.4 collective-permute-done.3
  682.7 0.1 copy.36
  682.7 0.1 copy.37
  682.8 2.1 scatter_fusion
  685.0 0.8 copy.38
  (26 shorter events, 0.2 us)
Async XLA Ops:
  7.2 184.1 %copy-start = (bf16[512,16]{0,1:T(8,128)(2,1)S(1)}, bf16[512,16]{0,1:T(8,128)(2,1)}, u32[]{:S(2)}) copy-start(bf16[512,16]{0,1:T(8,128)(2,1)} %param.10) | copy-start | bytes 49156
  7.2 94.7 %all-gather.3.cloned.1.call-start = ((), (), s32[]{:S(2)}) async-start(), calls=%async_computation.1 | async-start | bytes 1081344 | tf_op jit(solution)/shard_map/all_gather | solution.py:66
  7.9 183.3 %all-gather.5.cloned.1.call-start = ((), (), s32[]{:S(2)}) async-start(), calls=%async_computation.2 | async-start | bytes 1081344 | tf_op jit(solution)/shard_map/all_gather | solution.py:67
  11.3 12.8 %collective-permute-start = (bf16[16,128]{1,0:T(8,128)(2,1)S(1)}, bf16[16,128]{1,0:T(8,128)(2,1)S(1)}, u32[]{:S(2)}, u32[]{:S(2)}) collective-permute-start(bf16[16,128]{1,0:T(8,128)(2,1)S(1)} %get-tuple-element.28), channel_id=1, source_target_pairs={{0,32},{32,64},{64,96},{96,128},{128,160},{160,192},{192,224},{224... | collective-permute-start | bytes 12296 | tf_op jit(solution)/shard_map/ppermute | solution.py:15
  14.8 9.4 %collective-permute-start.1 = (bf16[16,128]{1,0:T(8,128)(2,1)S(1)}, bf16[16,128]{1,0:T(8,128)(2,1)S(1)}, u32[]{:S(2)}, u32[]{:S(2)}) collective-permute-start(bf16[16,128]{1,0:T(8,128)(2,1)S(1)} %get-tuple-element.29), channel_id=1, source_target_pairs={{32,0},{64,32},{96,64},{128,96},{160,128},{192,160},{224,192},{256... | collective-permute-start | bytes 12296 | tf_op jit(solution)/shard_map/ppermute | solution.py:18
  25.1 76.8 %copy-start.3 = (bf16[512,16]{0,1:T(8,128)(2,1)S(1)}, bf16[512,16]{0,1:T(8,128)(2,1)}, u32[]{:S(2)}) copy-start(bf16[512,16]{0,1:T(8,128)(2,1)} %param.9) | copy-start | bytes 49156
  25.1 166.1 %copy-start.4 = (bf16[16,1024]{1,0:T(8,128)(2,1)S(1)}, bf16[16,1024]{1,0:T(8,128)(2,1)}, u32[]{:S(2)}) copy-start(bf16[16,1024]{1,0:T(8,128)(2,1)} %param.11) | copy-start | bytes 98308
  88.2 260.8 %all-reduce.3.cloned.1.call-start = ((), (), s32[]{:S(2)}) async-start(), calls=%async_computation.4 | async-start | bytes 131072 | tf_op jit(solution)/shard_map/psum | solution.py:78
  101.9 94.8 %copy-start.1 = (bf16[512,1024]{1,0:T(8,128)(2,1)S(1)}, bf16[512,1024]{1,0:T(8,128)(2,1)}, u32[]{:S(2)}) copy-start(bf16[512,1024]{1,0:T(8,128)(2,1)} %all-gather.3.cloned.1.call-done) | copy-start | bytes 3145732
  191.2 4.5 copy-start.2
  197.7 381.2 %reduce-scatter.4.cloned.1.call-start = ((), (), s32[]{:S(2)}) async-start(), calls=%async_computation.3 | async-start | bytes 4325376
  207.2 0.7 copy-start.5
  672.6 7.7 %collective-permute-start.2 = (f32[16,128]{0,1:T(8,128)S(1)}, f32[16,128]{0,1:T(8,128)S(1)}, u32[]{:S(2)}, u32[]{:S(2)}) collective-permute-start(f32[16,128]{0,1:T(8,128)S(1)} %get-tuple-element.22), channel_id=1, source_target_pairs={{0,32},{32,64},{64,96},{96,128},{128,160},{160,192},{192,224},{224... | collective-permute-start | bytes 24584 | tf_op jit(solution)/shard_map/ppermute | solution.py:15
  679.0 3.7 collective-permute-start.3
Sparse Core Ops, SparseCore 0:
  11.8 90.1 all-gather.2
  106.2 84.9 all-gather.4
  197.9 151.0 all-reduce.2
  354.7 224.2 reduce-scatter.3
where the time goes:
time: 693 us; the launch traced here: 692 us
  waiting for transfers between devices  476 us (69%)
  other arithmetic  108 us (16%)
  local copies, waits for them, and re-layouts  69.7 us (10%)
  starting transfers between devices  17.1 us (2%)
  between operations  13.9 us (2%)
  matrix products  8.02 us (1%)
    unnamed x5, waiting for transfers between devices  229 us
    psum x1, waiting for transfers between devices, per_device(): grad_self, grad_neigh = lax.psum((self_part, neigh_part), 'dom')  141 us
    scatter-add x1, other arithmetic, spread_sum(): zeros_grid.at[:, neighbour_t].add(grad_block[:, None, :] * weights[None])  87.8 us
    all_gather x1, waiting for transfers between devices, per_device(): lax.all_gather(aggregate_rows, 'feat', axis=0, tiled=True)  87.8 us
    gather x1, local copies, waits for them, and re-layouts, gather_sum(): picked = extended[:, neighbour_t].astype(jnp.float32)  57.8 us
  transfers between devices with their start and end apart: 8, of which 6 were waited for; matrix products, arithmetic and copies ran while one was open for 12% of the time, Pallas kernels for 0%

commit v1 on v0

v1 whole, which is shorter than its diff:
```python
import functools
import math

import jax
import jax.numpy as jnp
from jax import lax
from jax.experimental import pallas as pl
from jax.experimental.pallas import tpu as pltpu
from jax.sharding import PartitionSpec as P

MESH = pl.DeviceIdType.MESH
BF16 = jnp.bfloat16
F32 = jnp.float32

HALO, XS, WS, COT, AGG, ACT, PART, GRAD, BACK, RS, AG, N_SEMS = range(12)


def dot(a, b):
    return jnp.dot(a, b, preferred_element_type=F32)


def dot_t(a, b):
    return lax.dot_general(a, b, (((1,), (1,)), ((), ())), preferred_element_type=F32)


def split_dot_t(a, b):
    high = a.astype(BF16)
    low = (a - high.astype(F32)).astype(BF16)
    both = dot_t(jnp.concatenate([high, low], axis=0), b)
    return both[: a.shape[0]] + both[a.shape[0] :]


def layer_kernel(
    sizes,
    x_ref, w1_ref, w2_ref, cot_ref, nb_ref, deg_ref, rows_ref, count_ref,
    act_ref, gx_ref, gs_ref, gn_ref,
    chosen, edges, ids, live,
    halo_out, halo_in, x_out, x_in, w_out, w_in, cot_out, cot_in, agg_out, agg_in,
    act_out, act_in, part_out, part_in, grad_out, grad_in, back_out, back_in,
    rs_out, rs_in, ag_in,
    send_sem, recv_sem,
):
    n_dom, n_y, n_x, width, block, halo, slots, eb = sizes
    n_feat = n_y * n_x
    nodes = n_y * block
    n_pieces = rs_out.shape[0]
    piece_w = rs_out.shape[2]
    lane_pieces = w1_ref.shape[1] // piece_w
    me_d = lax.axis_index("dom")
    me_f = lax.axis_index("feat")
    me_y = me_f // n_x
    me_x = me_f % n_x

    def remote(src, dst, which, dom, feat):
        return pltpu.make_async_remote_copy(
            src_ref=src, dst_ref=dst, send_sem=send_sem.at[which], recv_sem=recv_sem.at[which],
            device_id={"dom": dom, "feat": feat}, device_id_type=MESH,
        )

    def arrived(ref, which):
        remote(ref, ref, which, me_d, me_f).wait_recv()

    def sent(ref, which):
        remote(ref, ref, which, me_d, me_f).wait_send()

    def each(count, body):
        def step(i, carry):
            body(i)
            return carry
        lax.fori_loop(0, count, step, 0)

    def to_feat(body):
        def one(i):
            other = lax.rem(me_f + 1 + i, n_feat)
            body(other, other // n_x)
        each(n_feat - 1, one)

    def to_y(body):
        def one(i):
            other = lax.rem(me_y + 1 + i, n_y)
            body(other * n_x + me_x, other)
        each(n_y - 1, one)

    barrier = pltpu.get_barrier_semaphore()

    def greet_feat(other, _):
        pl.semaphore_signal(barrier, inc=1, device_id={"dom": me_d, "feat": other}, device_id_type=MESH)

    def greet_dom(i):
        other = lax.rem(me_d + 1 + i, n_dom)
        pl.semaphore_signal(barrier, inc=1, device_id={"dom": other, "feat": me_f}, device_id_type=MESH)

    to_feat(greet_feat)
    each(n_dom - 1, greet_dom)

    slot_id = lax.broadcasted_iota(jnp.int32, (1, 2 * halo), 1)
    limit = jnp.where(slot_id < halo, count_ref[0], count_ref[1] + halo)
    rows = jnp.concatenate([rows_ref[0:1, :], rows_ref[1:2, :]], axis=1)
    rows = jnp.where(slot_id < limit, rows, -1)
    node_id = lax.broadcasted_iota(jnp.int32, (nodes, 2 * halo), 0)
    chosen[...] = jnp.where(node_id == rows, 1.0, 0.0).astype(BF16)
    x = x_ref[...]
    picked = dot(x, chosen[...]).astype(BF16)
    halo_out[0] = picked[:, :halo]
    halo_out[1] = picked[:, halo:]
    for y in range(n_y):
        x_out[y] = x[:, y * block : (y + 1) * block]
        cot_out[y] = cot_ref[:, y * block : (y + 1) * block]
    w_out[0] = w1_ref[...]
    w_out[1] = w2_ref[...]
    x_in[me_f] = x_out[me_y]
    cot_in[me_y] = cot_out[me_y]
    w_in[me_y] = w_out[...]

    pl.semaphore_wait(barrier, n_feat - 1 + n_dom - 1)

    before = lax.rem(me_d + n_dom - 1, n_dom)
    after = lax.rem(me_d + 1, n_dom)
    remote(halo_out.at[0], halo_in.at[1], HALO, before, me_f).start()
    remote(halo_out.at[1], halo_in.at[0], HALO, after, me_f).start()
    to_feat(lambda f, y: remote(x_out.at[y], x_in.at[me_f], XS, me_d, f).start())
    to_y(lambda f, y: remote(w_out, w_in.at[me_y], WS, me_d, f).start())
    to_y(lambda f, y: remote(cot_out.at[y], cot_in.at[me_y], COT, me_d, f).start())

    degree = deg_ref[...]
    slot = lax.broadcasted_iota(jnp.int32, (slots, nodes), 0)
    live[...] = jnp.where(slot < degree, nb_ref[...], -1)
    ids[...] = lax.broadcasted_iota(jnp.int32, (eb, block), 0).astype(F32).astype(BF16)
    inverse = 1.0 / degree.astype(F32)

    def count_edges(t):
        lanes = pl.ds(pl.multiple_of((t % n_y) * block, block), block)
        base = (t // n_y) * eb
        mine = (live[:, lanes] - base).astype(F32).astype(BF16)
        known = ids[...]
        total = jnp.zeros((eb, block), BF16)
        for k in range(slots):
            total = total + jnp.where(known == mine[k : k + 1, :], jnp.ones((), BF16), jnp.zeros((), BF16))
        edges[pl.ds(pl.multiple_of(base, eb), eb), lanes] = total

    each((nodes + 2 * halo) // eb * n_y, count_edges)

    mean = dot(x, edges[:nodes, :])
    arrived(halo_in, HALO)
    mean += dot(halo_in[0], edges[nodes : nodes + halo, :])
    mean += dot(halo_in[1], edges[nodes + halo :, :])
    mean = (mean * inverse).astype(BF16)
    for y in range(n_y):
        agg_out[y] = mean[:, y * block : (y + 1) * block]
    to_feat(lambda f, y: remote(agg_out.at[y], agg_in.at[me_f], AGG, me_d, f).start())
    agg_in[me_f] = agg_out[me_y]

    wide = w1_ref.shape[1]
    quarter = n_y * width
    arrived(w_in.at[pl.ds(0, n_y - 1)], WS)
    arrived(x_in.at[pl.ds(0, n_feat - 1)], XS)
    w1 = w_in[:, 0].reshape(quarter, wide)
    w2 = w_in[:, 1].reshape(quarter, wide)
    full_x = x_in[...].reshape(wide, block)
    preact = dot(w1, full_x)
    w1_t = w1.T
    w2_t = w2.T
    arrived(cot_in.at[pl.ds(0, n_y - 1)], COT)
    cot = cot_in[...].reshape(quarter, block).astype(F32)
    arrived(agg_in.at[pl.ds(0, n_feat - 1)], AGG)
    full_agg = agg_in[...].reshape(wide, block)
    preact += dot(w2, full_agg)
    s = jax.nn.sigmoid(preact)
    grad = (cot * s * (1.0 + preact * (1.0 - s))).astype(BF16)
    part_out[:, 0] = dot(w1_t, grad).astype(BF16).reshape(n_feat, width, block)
    part_out[:, 1] = dot(w2_t, grad).astype(BF16).reshape(n_feat, width, block)
    to_feat(lambda f, y: remote(part_out.at[f], part_in.at[me_f], PART, me_d, f).start())
    part_in[me_f] = part_out[me_f]

    grad_out[:, 0] = dot_t(grad, full_x).reshape(n_y, width, wide)
    grad_out[:, 1] = dot_t(grad, full_agg).reshape(n_y, width, wide)
    to_y(lambda f, y: remote(grad_out.at[y], grad_in.at[me_y], GRAD, me_d, f).start())
    grad_in[me_y] = grad_out[me_y]

    act_out[...] = (preact * s).astype(BF16).reshape(n_y, width, block)
    to_y(lambda f, y: remote(act_out.at[y], act_in.at[me_y], ACT, me_d, f).start())
    act_in[me_y] = act_out[me_y]

    arrived(part_in.at[pl.ds(0, n_feat - 1)], PART)
    direct, spread = [], []
    for y in range(n_y):
        here = part_in[pl.ds(y * n_x, n_x)].astype(F32)
        here = jnp.sum(here, axis=0)
        direct.append(here[0])
        spread.append(here[1])
    direct = jnp.concatenate(direct, axis=1)
    spread = jnp.concatenate(spread, axis=1) * inverse
    ext = split_dot_t(spread, edges[nodes:, :])
    back_out[0] = ext[:, :halo]
    back_out[1] = ext[:, halo:]
    remote(back_out.at[0], back_in.at[1], BACK, before, me_f).start()
    remote(back_out.at[1], back_in.at[0], BACK, after, me_f).start()

    arrived(grad_in.at[pl.ds(0, n_y - 1)], GRAD)
    weight_grad = jnp.sum(grad_in[...], axis=0)
    for piece in range(n_pieces):
        row, lane = piece // lane_pieces, piece % lane_pieces
        which, row = row // (width // 8), row % (width // 8)
        rs_out[piece] = weight_grad[which, row * 8 : (row + 1) * 8, lane * piece_w : (lane + 1) * piece_w]

    def scatter(i):
        other = lax.rem(me_d + 1 + i, n_dom)

        @pl.when(other < n_pieces)
        def _():
            remote(rs_out.at[other], rs_in.at[me_d], RS, other, me_f).start()

    each(n_dom - 1, scatter)

    gx = direct + split_dot_t(spread, edges[:nodes, :])

    @pl.when(me_d < n_pieces)
    def _():
        rs_in[me_d] = rs_out[me_d]
        arrived(rs_in.at[pl.ds(0, n_dom - 1)], RS)
        ag_in[me_d] = jnp.sum(rs_in[...], axis=0) * (1.0 / math.sqrt(nodes * n_dom))

        def give(i):
            other = lax.rem(me_d + 1 + i, n_dom)
            remote(ag_in.at[me_d], ag_in.at[me_d], AG, other, me_f).start()

        each(n_dom - 1, give)

    arrived(back_in, BACK)
    gx += split_dot_t(jnp.concatenate([back_in[0], back_in[1]], axis=1), chosen[...])
    gx_ref[...] = gx

    arrived(act_in.at[pl.ds(0, n_y - 1)], ACT)
    for y in range(n_y):
        act_ref[:, y * block : (y + 1) * block] = act_in[y]

    sent(halo_out, HALO)
    sent(x_in.at[pl.ds(0, n_feat - 1)], XS)
    sent(w_in.at[pl.ds(0, n_y - 1)], WS)
    sent(cot_in.at[pl.ds(0, n_y - 1)], COT)
    sent(agg_in.at[pl.ds(0, n_feat - 1)], AGG)
    sent(part_in.at[pl.ds(0, n_feat - 1)], PART)
    sent(grad_in.at[pl.ds(0, n_y - 1)], GRAD)
    sent(act_in.at[pl.ds(0, n_y - 1)], ACT)
    sent(back_out, BACK)

    @pl.when(me_d < n_pieces)
    def _():
        sent(rs_out.at[pl.ds(0, n_pieces - 1)], RS)
        sent(rs_in.at[pl.ds(0, n_dom - 1)], AG)
        arrived(ag_in.at[pl.ds(0, n_pieces - 1)], AG)

    @pl.when(me_d >= n_pieces)
    def _():
        sent(rs_out, RS)
        arrived(ag_in, AG)

    for piece in range(n_pieces):
        row, lane = piece // lane_pieces, piece % lane_pieces
        which, row = row // (width // 8), row % (width // 8)
        ref = gs_ref if which == 0 else gn_ref
        ref[row * 8 : (row + 1) * 8, lane * piece_w : (lane + 1) * piece_w] = ag_in[piece]


def per_device(
    n_x, features, self_weight, neigh_weight, cotangent, neighbours, degrees, send_rows, send_count
):
    width, nodes = features.shape
    wide = self_weight.shape[0]
    slots = neighbours.shape[1]
    halo = send_rows.shape[1]
    n_dom = lax.axis_size("dom")
    n_feat = lax.axis_size("feat")
    n_y = n_feat // n_x
    block = nodes // n_y
    eb = min(256, 2 * halo)
    piece_w = min(128, wide)
    n_pieces = 2 * (width // 8) * (wide // piece_w)
    sizes = (n_dom, n_y, n_x, width, block, halo, slots, eb)
    vmem = pl.BlockSpec(memory_space=pltpu.VMEM)
    tile = lambda *lead: pltpu.VMEM((*lead, width, block), BF16)
    act, gx, gs, gn = pl.pallas_call(
        functools.partial(layer_kernel, sizes),
        out_shape=(
            jax.ShapeDtypeStruct((width, nodes), BF16),
            jax.ShapeDtypeStruct((width, nodes), F32),
            jax.ShapeDtypeStruct((width, wide), F32),
            jax.ShapeDtypeStruct((width, wide), F32),
        ),
        in_specs=[vmem] * 7 + [pl.BlockSpec(memory_space=pltpu.SMEM)],
        out_specs=(vmem,) * 4,
        scratch_shapes=[
            pltpu.VMEM((nodes, 2 * halo), BF16),
            pltpu.VMEM((nodes + 2 * halo, nodes), BF16),
            pltpu.VMEM((eb, block), BF16),
            pltpu.VMEM((slots, nodes), jnp.int32),
            pltpu.VMEM((2, width, halo), BF16),
            pltpu.VMEM((2, width, halo), BF16),
            tile(n_y), tile(n_feat),
            pltpu.VMEM((2, width, wide), BF16),
            pltpu.VMEM((n_y, 2, width, wide), BF16),
            tile(n_y), tile(n_y),
            tile(n_y), tile(n_feat),
            tile(n_y), tile(n_y),
            tile(n_feat, 2), tile(n_feat, 2),
            pltpu.VMEM((n_y, 2, width, wide), F32),
            pltpu.VMEM((n_y, 2, width, wide), F32),
            pltpu.VMEM((2, width, halo), F32),
            pltpu.VMEM((2, width, halo), F32),
            pltpu.VMEM((n_pieces, 8, piece_w), F32),
            pltpu.VMEM((n_dom, 8, piece_w), F32),
            pltpu.VMEM((n_pieces, 8, piece_w), F32),
            pltpu.SemaphoreType.DMA((N_SEMS,)),
            pltpu.SemaphoreType.DMA((N_SEMS,)),
        ],
        compiler_params=pltpu.CompilerParams(
            collective_id=0, has_side_effects=True, vmem_limit_bytes=32 * 1024 * 1024
        ),
    )(
        features, self_weight.T, neigh_weight.T, cotangent, neighbours.T, degrees.reshape(1, nodes),
        send_rows, send_count,
    )
    return act, gx, gs.T, gn.T


def solution(mesh):
    n_x = 4 if mesh.shape["feat"] % 4 == 0 and mesh.shape["feat"] > 4 else 2
    return jax.shard_map(
        functools.partial(per_device, n_x),
        mesh=mesh,
        in_specs=(
            P("feat", "dom"),
            P(None, "feat"),
            P(None, "feat"),
            P("feat", "dom"),
            P("dom", None),
            P("dom"),
            P("dom", None),
            P("dom"),
        ),
        out_specs=(P("feat", "dom"), P("feat", "dom"), P(None, "feat"), P(None, "feat")),
        check_vma=False,
    )
```

time: 693 us -> 79 us (0.11)
  waiting for transfers between devices: 476 us -> 0 us
  other arithmetic: 108 us -> 0 us
  Pallas kernels: 0 us -> 70.9 us
  local copies, waits for them, and re-layouts: 69.7 us -> 6.94 us
  starting transfers between devices: 17.1 us -> 0 us
  between operations: 13.9 us -> 0.67 us
  matrix products: 8.02 us -> 0 us
    unnamed x5 -> x0, waiting for transfers between devices: 229 us -> none
    psum x1 -> x0, waiting for transfers between devices: 141 us -> none  [per_device(): grad_self, grad_neigh = lax.psum((self_part, neigh_part), 'dom')]
    all_gather x2 -> x0, waiting for transfers between devices: 101 us -> none  [the longest x1 87.8 us: per_device(): lax.all_gather(aggregate_rows, 'feat', axis=0, tiled=True)]
    scatter-add x2 -> x0, other arithmetic: 89.9 us -> none  [the longest x1 87.8 us: spread_sum(): zeros_grid.at[:, neighbour_t].add(grad_block[:, None, :] * weights[None])]
    pallas_call x0 -> x1, Pallas kernels: none -> 70.9 us  [per_device(): pl.pallas_call(functools.partial(layer_kernel, sizes), out_shape=(jax.Sha...]
    gather x3 -> x0, local copies, waits for them, and re-layouts: 58.7 us -> none  [the longest x1 57.8 us: gather_sum(): picked = extended[:, neighbour_t].astype(jnp.float32)]
    ppermute x4 -> x0, starting transfers between devices: 16.9 us -> none  [the longest x2 9.83 us: extended_2(): lax.ppermute(lax.slice_in_dim(block, block.shape[dim] - width, None, axis...]
    dot_general x6 -> x0, matrix products: 8.02 us -> none  [the longest x2 3.76 us: contract_first(): lax.dot_general(weight_block, columns, (((0,), (0,)), ((), ())), preferre...]
  transfers between devices with their start and end apart: 8 -> 0, of which waited for: 6 -> 0; matrix products, arithmetic and copies ran while one was open for 12% -> 0% of each run, Pallas kernels for 0% -> 0%
where the time goes in v1:
time: 79 us; the launch traced here: 78.5 us
  Pallas kernels  70.9 us (90%)
  local copies, waits for them, and re-layouts  6.94 us (9%)
    pallas_call x1, Pallas kernels, per_device(): pl.pallas_call(functools.partial(layer_kernel, sizes), out_shape=(jax.Sha...  70.9 us
    unnamed x20, local copies, waits for them, and re-layouts  6.94 us

profile of v1, /device:TPU:1, one launch (start us, length us, event | category | flops | bytes accessed | tf_op | source)
XLA Modules:
  0.0 78.5 jit_solution(859293261319925648)
XLA Ops:
  0.6 0.0 copy-start.5
  0.6 0.0 copy-start.6
  0.7 0.0 copy-start.7
  0.7 0.7 copy-done.5
  1.3 0.0 copy-done.6
  1.3 0.0 copy-done.7
  1.3 0.0 copy-start
  1.3 0.8 %copy-done = s32[1024,16]{0,1:T(8,128)S(1)} copy-done((s32[1024,16]{0,1:T(8,128)S(1)}, s32[1024,16]{0,1:T(8,128)}, u32[]{:S(2)}) %copy-start) | copy-done | bytes 65560
  2.2 0.0 copy-start.1
  2.2 0.8 copy-done.1
  2.9 0.0 copy-start.2
  2.9 0.8 copy-done.2
  3.7 0.0 copy-start.3
  3.7 0.7 copy-done.3
  4.4 0.0 copy-start.4
  4.4 0.7 copy-done.4
  5.1 70.9 %shard_map.111 = (bf16[16,1024]{1,0:T(8,128)(2,1)S(1)}, f32[16,1024]{1,0:T(8,128)S(1)}, f32[16,512]{1,0:T(8,128)S(1)}, f32[16,512]{1,0:T(8,128)S(1)}) custom-call(bf16[16,1024]{1,0:T(8,128)(2,1)S(1)} %copy-done.1, bf16[16,512]{1,0:T(8,128)(2,1)S(1)} %bitcast.9, bf16[16,512]{1,0:T(8,128)(2,1)S(1)} %bitcast.10, bf16[16,1024]{1,0:T(8,128)(2,1)S(1)} %copy-done.2, ...), custom_call_target="tpu_custom_call" | custom-call | tf_op jit(solution)/shard_map/pallas_call | solution.py:282
  76.0 0.6 copy.16
  76.7 0.6 copy.17
  77.3 0.6 copy.18
  77.9 0.6 copy.19
Async XLA Ops:
  0.6 0.7 copy-start.5
  0.6 0.7 copy-start.6
  0.7 0.7 copy-start.7
  1.3 0.8 %copy-start = (s32[1024,16]{0,1:T(8,128)S(1)}, s32[1024,16]{0,1:T(8,128)}, u32[]{:S(2)}) copy-start(s32[1024,16]{0,1:T(8,128)} %param.12) | copy-start | bytes 196612
  2.2 0.8 copy-start.1
  2.9 0.8 copy-start.2
  3.7 0.7 copy-start.3
  4.4 0.7 copy-start.4

commit v2 on v1

v2 whole, which is shorter than its diff:
```python
import functools
import math

import jax
import jax.numpy as jnp
from jax import lax
from jax.experimental import pallas as pl
from jax.experimental.pallas import tpu as pltpu
from jax.sharding import PartitionSpec as P

MESH = pl.DeviceIdType.MESH
BF16 = jnp.bfloat16
F32 = jnp.float32

HALO, XS, WS, WMATE, COT, AGG, ACT, PART, PAIR, GRAD, BACK, ACROSS, LAST, N_SEMS = range(14)
IN_X, IN_W1, IN_W2, IN_COT, IN_NB, IN_DEG, IN_ROWS, N_IN = range(8)


def dot(a, b):
    return jnp.dot(a, b, preferred_element_type=F32)


def dot_t(a, b):
    return lax.dot_general(a, b, (((1,), (1,)), ((), ())), preferred_element_type=F32)


def split_dot_t(a, b):
    high = a.astype(BF16)
    low = (a - high.astype(F32)).astype(BF16)
    both = dot_t(jnp.concatenate([high, low], axis=0), b)
    return both[: a.shape[0]] + both[a.shape[0] :]


def layer_kernel(
    sizes,
    x_hbm, w1_hbm, w2_hbm, cot_hbm, nb_hbm, deg_hbm, rows_hbm, count_ref,
    act_ref, gx_ref, gs_ref, gn_ref,
    x_ref, w_ref, cot_ref, nb_ref, deg_ref, rows_ref,
    chosen, edges, ids, live,
    halo_out, halo_in, x_out, x_in, w_in, w_mate, cot_out, cot_in, agg_out, agg_in,
    act_out, act_in, part_out, part_in, pair_out, pair_in, grad_out, grad_in, back_out, back_in,
    across_out, across_in, sums,
    send_sem, recv_sem, in_sem,
):
    n_dom, n_y, n_x, width, block, halo, slots, eb = sizes
    n_feat = n_y * n_x
    n_z = n_dom // 2
    nodes = n_y * block
    wide = w1_hbm.shape[1]
    me_d = lax.axis_index("dom")
    me_f = lax.axis_index("feat")
    me_y = me_f // n_x
    me_x = me_f % n_x
    me_z = me_d // 2
    core = me_d % 2
    mate = me_d + 1 - 2 * core
    before = lax.rem(me_d + n_dom - 1, n_dom)
    after = lax.rem(me_d + 1, n_dom)
    far = jnp.where(core == 0, before, after)

    loads = {}
    for which, src, dst in (
        (IN_X, x_hbm, x_ref), (IN_ROWS, rows_hbm, rows_ref), (IN_W1, w1_hbm, w_ref.at[0]), (IN_W2, w2_hbm, w_ref.at[1]),
        (IN_COT, cot_hbm, cot_ref), (IN_NB, nb_hbm, nb_ref), (IN_DEG, deg_hbm, deg_ref),
    ):
        loads[which] = pltpu.make_async_copy(src, dst, in_sem.at[which])
        loads[which].start()

    def remote(src, dst, which, dom, feat):
        return pltpu.make_async_remote_copy(
            src_ref=src, dst_ref=dst, send_sem=send_sem.at[which], recv_sem=recv_sem.at[which],
            device_id={"dom": dom, "feat": feat}, device_id_type=MESH,
        )

    def arrived(ref, which):
        remote(ref, ref, which, me_d, me_f).wait_recv()

    def sent(ref, which):
        remote(ref, ref, which, me_d, me_f).wait_send()

    def each(count, body):
        def step(i, carry):
            body(i)
            return carry
        lax.fori_loop(0, count, step, 0)

    def to_feat(body):
        def one(i):
            other = lax.rem(me_f + 1 + i, n_feat)
            body(other, other // n_x)
        each(n_feat - 1, one)

    def to_y(body):
        def one(i):
            other = lax.rem(me_y + 1 + i, n_y)
            body(other * n_x + me_x, other)
        each(n_y - 1, one)

    barrier = pltpu.get_barrier_semaphore()

    def greet(dom, feat):
        pl.semaphore_signal(barrier, inc=1, device_id={"dom": dom, "feat": feat}, device_id_type=MESH)

    def to_z(body):
        def one(i):
            other = lax.rem(me_z + 1 + i, n_z)
            body(other * 2 + core, other)
        each(n_z - 1, one)

    greet(far, me_f)
    greet(mate, me_f)
    to_feat(lambda f, y: greet(me_d, f))
    to_z(lambda d, z: greet(d, me_f))

    slot_id = lax.broadcasted_iota(jnp.int32, (1, 2 * halo), 1)
    limit = jnp.where(slot_id < halo, count_ref[0], count_ref[1] + halo)
    loads[IN_ROWS].wait()
    rows = jnp.concatenate([rows_ref[0:1, :], rows_ref[1:2, :]], axis=1)
    rows = jnp.where(slot_id < limit, rows, -1)
    node_id = lax.broadcasted_iota(jnp.int32, (nodes, 2 * halo), 0)
    chosen[...] = jnp.where(node_id == rows, 1.0, 0.0).astype(BF16)
    loads[IN_X].wait()
    x = x_ref[...]
    picked = dot(x, chosen[...]).astype(BF16)
    halo_out[0] = picked[:, :halo]
    halo_out[1] = picked[:, halo:]
    loads[IN_COT].wait()
    for y in range(n_y):
        x_out[y] = x[:, y * block : (y + 1) * block]
        cot_out[y] = cot_ref[:, y * block : (y + 1) * block]
    x_in[me_f] = x_out[me_y]
    cot_in[me_y] = cot_out[me_y]
    loads[IN_W1].wait()
    loads[IN_W2].wait()
    w_in[me_y] = w_ref[core]

    pl.semaphore_wait(barrier, n_feat - 1 + n_z - 1 + 2)

    remote(halo_out.at[0], halo_in.at[1], HALO, before, me_f).start()
    remote(halo_out.at[1], halo_in.at[0], HALO, after, me_f).start()
    to_y(lambda f, y: remote(w_ref.at[core], w_in.at[me_y], WS, me_d, f).start())
    to_feat(lambda f, y: remote(x_out.at[y], x_in.at[me_f], XS, me_d, f).start())
    to_y(lambda f, y: remote(cot_out.at[y], cot_in.at[me_y], COT, me_d, f).start())

    loads[IN_DEG].wait()
    loads[IN_NB].wait()
    degree = deg_ref[...]
    slot = lax.broadcasted_iota(jnp.int32, (slots, nodes), 0)
    live[...] = jnp.where(slot < degree, nb_ref[...], -1)
    ids[...] = lax.broadcasted_iota(jnp.int32, (eb, block), 0).astype(F32).astype(BF16)
    inverse = 1.0 / degree.astype(F32)

    def count_edges(t):
        lanes = pl.ds(pl.multiple_of((t % n_y) * block, block), block)
        base = (t // n_y) * eb
        mine = (live[:, lanes] - base).astype(F32).astype(BF16)
        known = ids[...]
        total = jnp.zeros((eb, block), BF16)
        for k in range(slots):
            total = total + jnp.where(known == mine[k : k + 1, :], jnp.ones((), BF16), jnp.zeros((), BF16))
        edges[pl.ds(pl.multiple_of(base, eb), eb), lanes] = total

    each((nodes + 2 * halo) // eb * n_y, count_edges)

    mean = dot(x, edges[:nodes, :])
    arrived(halo_in, HALO)
    mean += dot(halo_in[0], edges[nodes : nodes + halo, :])
    mean += dot(halo_in[1], edges[nodes + halo :, :])
    mean = (mean * inverse).astype(BF16)
    for y in range(n_y):
        agg_out[y] = mean[:, y * block : (y + 1) * block]
    to_feat(lambda f, y: remote(agg_out.at[y], agg_in.at[me_f], AGG, me_d, f).start())
    agg_in[me_f] = agg_out[me_y]

    quarter = n_y * width
    arrived(w_in.at[pl.ds(0, n_y - 1)], WS)
    remote(w_in, w_mate, WMATE, mate, me_f).start()
    arrived(x_in.at[pl.ds(0, n_feat - 1)], XS)
    full_x = x_in[...].reshape(wide, block)
    arrived(w_mate, WMATE)
    own_w = w_in[...].reshape(quarter, wide)
    other_w = w_mate[...].reshape(quarter, wide)
    w1 = jnp.where(core == 0, own_w, other_w)
    w2 = jnp.where(core == 0, other_w, own_w)
    preact = dot(w1, full_x)
    w1_t = w1.T
    w2_t = w2.T
    arrived(cot_in.at[pl.ds(0, n_y - 1)], COT)
    cot = cot_in[...].reshape(quarter, block).astype(F32)
    arrived(agg_in.at[pl.ds(0, n_feat - 1)], AGG)
    full_agg = agg_in[...].reshape(wide, block)
    preact += dot(w2, full_agg)
    s = jax.nn.sigmoid(preact)
    grad = (cot * s * (1.0 + preact * (1.0 - s))).astype(BF16)
    pair_out[0] = dot_t(grad, full_x)
    pair_out[1] = dot_t(grad, full_agg)
    remote(pair_out.at[1 - core], pair_in, PAIR, mate, me_f).start()

    part_out[:, 0] = dot(w1_t, grad).astype(BF16).reshape(n_feat, width, block)
    part_out[:, 1] = dot(w2_t, grad).astype(BF16).reshape(n_feat, width, block)
    part_in[me_f] = part_out[me_f]

    arrived(pair_in, PAIR)
    grad_out[...] = (pair_out[core] + pair_in[...]).astype(BF16).reshape(n_y, width, wide)
    to_y(lambda f, y: remote(grad_out.at[y], grad_in.at[me_y], GRAD, me_d, f).start())
    grad_in[me_y] = grad_out[me_y]
    to_feat(lambda f, y: remote(part_out.at[f], part_in.at[me_f], PART, me_d, f).start())

    act_out[...] = (preact * s).astype(BF16).reshape(n_y, width, block)
    to_y(lambda f, y: remote(act_out.at[y], act_in.at[me_y], ACT, me_d, f).start())
    act_in[me_y] = act_out[me_y]

    arrived(grad_in.at[pl.ds(0, n_y - 1)], GRAD)
    across_out[...] = jnp.sum(grad_in[...].astype(F32), axis=0).astype(BF16)
    to_z(lambda d, z: remote(across_out, across_in.at[me_z], ACROSS, d, me_f).start())
    across_in[me_z] = across_out[...]

    arrived(part_in.at[pl.ds(0, n_feat - 1)], PART)
    direct, spread = [], []
    for y in range(n_y):
        here = part_in[pl.ds(y * n_x, n_x)].astype(F32)
        here = jnp.sum(here, axis=0)
        direct.append(here[0])
        spread.append(here[1])
    direct = jnp.concatenate(direct, axis=1)
    spread = jnp.concatenate(spread, axis=1) * inverse
    ext = split_dot_t(spread, edges[nodes:, :])
    back_out[0] = ext[:, :halo]
    back_out[1] = ext[:, halo:]
    remote(back_out.at[0], back_in.at[1], BACK, before, me_f).start()
    remote(back_out.at[1], back_in.at[0], BACK, after, me_f).start()

    gx = direct + split_dot_t(spread, edges[:nodes, :])

    arrived(back_in, BACK)
    gx += split_dot_t(jnp.concatenate([back_in[0], back_in[1]], axis=1), chosen[...])
    gx_ref[...] = gx

    arrived(act_in.at[pl.ds(0, n_y - 1)], ACT)
    for y in range(n_y):
        act_ref[:, y * block : (y + 1) * block] = act_in[y]

    arrived(across_in.at[pl.ds(0, n_z - 1)], ACROSS)
    sums[core] = jnp.sum(across_in[...].astype(F32), axis=0) * (1.0 / math.sqrt(nodes * n_dom))
    last = remote(sums.at[core], sums.at[core], LAST, mate, me_f)
    last.start()

    sent(halo_out, HALO)
    sent(w_in.at[pl.ds(0, n_y - 1)], WS)
    sent(w_in, WMATE)
    sent(x_in.at[pl.ds(0, n_feat - 1)], XS)
    sent(cot_in.at[pl.ds(0, n_y - 1)], COT)
    sent(agg_in.at[pl.ds(0, n_feat - 1)], AGG)
    sent(pair_in, PAIR)
    sent(part_in.at[pl.ds(0, n_feat - 1)], PART)
    sent(grad_in.at[pl.ds(0, n_y - 1)], GRAD)
    sent(act_in.at[pl.ds(0, n_y - 1)], ACT)
    sent(back_out, BACK)
    sent(across_in.at[pl.ds(0, n_z - 1)], ACROSS)
    last.wait()
    gs_ref[...] = sums[0]
    gn_ref[...] = sums[1]


def hand_over(*refs):
    for src, dst in zip(refs[:4], refs[4:]):
        dst[...] = src[...]


def per_device(
    n_x, features, self_weight, neigh_weight, cotangent, neighbours, degrees, send_rows, send_count
):
    width, nodes = features.shape
    wide = self_weight.shape[0]
    slots = neighbours.shape[1]
    halo = send_rows.shape[1]
    n_dom = lax.axis_size("dom")
    n_feat = lax.axis_size("feat")
    n_y = n_feat // n_x
    block = nodes // n_y
    eb = min(256, 2 * halo)
    sizes = (n_dom, n_y, n_x, width, block, halo, slots, eb)
    vmem = pl.BlockSpec(memory_space=pltpu.VMEM)
    tile = lambda *lead: pltpu.VMEM((*lead, width, block), BF16)
    act, gx, gs, gn = pl.pallas_call(
        functools.partial(layer_kernel, sizes),
        out_shape=(
            jax.ShapeDtypeStruct((width, nodes), BF16),
            jax.ShapeDtypeStruct((width, nodes), F32),
            jax.ShapeDtypeStruct((width, wide), F32),
            jax.ShapeDtypeStruct((width, wide), F32),
        ),
        in_specs=[pl.BlockSpec(memory_space=pltpu.HBM)] * 7 + [pl.BlockSpec(memory_space=pltpu.SMEM)],
        out_specs=(vmem,) * 4,
        scratch_shapes=[
            pltpu.VMEM((width, nodes), BF16),
            pltpu.VMEM((2, width, wide), BF16),
            pltpu.VMEM((width, nodes), BF16),
            pltpu.VMEM((slots, nodes), jnp.int32),
            pltpu.VMEM((1, nodes), jnp.int32),
            pltpu.VMEM((2, halo), jnp.int32),
            pltpu.VMEM((nodes, 2 * halo), BF16),
            pltpu.VMEM((nodes + 2 * halo, nodes), BF16),
            pltpu.VMEM((eb, block), BF16),
            pltpu.VMEM((slots, nodes), jnp.int32),
            pltpu.VMEM((2, width, halo), BF16),
            pltpu.VMEM((2, width, halo), BF16),
            tile(n_y), tile(n_feat),
            pltpu.VMEM((n_y, width, wide), BF16),
            pltpu.VMEM((n_y, width, wide), BF16),
            tile(n_y), tile(n_y),
            tile(n_y), tile(n_feat),
            tile(n_y), tile(n_y),
            tile(n_feat, 2), tile(n_feat, 2),
            pltpu.VMEM((2, n_y * width, wide), F32),
            pltpu.VMEM((n_y * width, wide), F32),
            pltpu.VMEM((n_y, width, wide), BF16),
            pltpu.VMEM((n_y, width, wide), BF16),
            pltpu.VMEM((2, width, halo), F32),
            pltpu.VMEM((2, width, halo), F32),
            pltpu.VMEM((width, wide), BF16),
            pltpu.VMEM((n_dom // 2, width, wide), BF16),
            pltpu.VMEM((2, width, wide), F32),
            pltpu.SemaphoreType.DMA((N_SEMS,)),
            pltpu.SemaphoreType.DMA((N_SEMS,)),
            pltpu.SemaphoreType.DMA((N_IN,)),
        ],
        compiler_params=pltpu.CompilerParams(
            collective_id=0, has_side_effects=True, vmem_limit_bytes=64 * 1024 * 1024
        ),
    )(
        features, self_weight.T, neigh_weight.T, cotangent, neighbours.T, degrees.reshape(1, nodes),
        send_rows, send_count,
    )
    act, gx, gs, gn = pl.pallas_call(
        hand_over,
        out_shape=tuple(jax.ShapeDtypeStruct(a.shape, a.dtype) for a in (act, gx, gs, gn)),
        in_specs=[vmem] * 4,
        out_specs=(vmem,) * 4,
    )(act, gx, gs, gn)
    return act, gx, gs.T, gn.T


def solution(mesh):
    n_x = 4 if mesh.shape["feat"] % 4 == 0 and mesh.shape["feat"] > 4 else 2
    return jax.shard_map(
        functools.partial(per_device, n_x),
        mesh=mesh,
        in_specs=(
            P("feat", "dom"),
            P(None, "feat"),
            P(None, "feat"),
            P("feat", "dom"),
            P("dom", None),
            P("dom"),
            P("dom", None),
            P("dom"),
        ),
        out_specs=(P("feat", "dom"), P("feat", "dom"), P(None, "feat"), P(None, "feat")),
        check_vma=False,
    )
```

time: 79 us -> 60.5 us (0.77)
  Pallas kernels: 70.9 us -> 59.6 us
  local copies, waits for them, and re-layouts: 6.94 us -> 0 us
    pallas_call x1, Pallas kernels: 70.9 us -> 58.1 us  [per_device(): pl.pallas_call(functools.partial(layer_kernel, sizes), out_shape=(jax.Sha...]
    unnamed x20 -> x0, local copies, waits for them, and re-layouts: 6.94 us -> none
    pallas_call x0 -> x1, Pallas kernels: none -> 1.51 us  [per_device(): pl.pallas_call(hand_over, out_shape=tuple((jax.ShapeDtypeStruct(a.shape,...]
where the time goes in v2:
time: 60.5 us; the launch traced here: 60.3 us
  Pallas kernels  59.6 us (99%)
  between operations  0.64 us (1%)
    pallas_call x1, Pallas kernels, per_device(): pl.pallas_call(functools.partial(layer_kernel, sizes), out_shape=(jax.Sha...  58.1 us
    pallas_call x1, Pallas kernels, per_device(): pl.pallas_call(hand_over, out_shape=tuple((jax.ShapeDtypeStruct(a.shape,...  1.51 us

profile of v2, /device:TPU:1, one launch (start us, length us, event | category | flops | bytes accessed | tf_op | source)
XLA Modules:
  0.0 60.3 jit_solution(16154834098503305428)
XLA Ops:
  0.6 58.1 %shard_map.111 = (bf16[16,1024]{1,0:T(8,128)(2,1)}, f32[16,1024]{1,0:T(8,128)}, f32[16,512]{1,0:T(8,128)}, f32[16,512]{1,0:T(8,128)}) custom-call(bf16[16,1024]{1,0:T(8,128)(2,1)} %x_hbm.1, bf16[16,512]{1,0:T(8,128)(2,1)} %bitcast.7, bf16[16,512]{1,0:T(8,128)(2,1)} %bitcast.8, bf16[16,1024]{1,0:T(8,128)(2,1)} %cot_hbm.1, s32[16,1024]{1,0:T(8,128)} %bitcast.6, ...), custom_call_target="tpu_custom_call" | custom-call | tf_op jit(solution)/shard_map/pallas_call | solution.py:285
  58.8 1.5 %shard_map.112 = (bf16[16,1024]{1,0:T(8,128)(2,1)}, f32[16,1024]{1,0:T(8,128)}, f32[16,512]{1,0:T(8,128)}, f32[16,512]{1,0:T(8,128)}) custom-call(bf16[16,1024]{1,0:T(8,128)(2,1)} %get-tuple-element.12.refs_0_, f32[16,1024]{1,0:T(8,128)} %get-tuple-element.13.refs_1_, f32[16,512]{1,0:T(8,128)} %get-tuple-element.14.refs_2_, f32[16,512]{1,0:T(8,128)} %get-tuple-element.15.refs_3_), custom_call_target="tpu_custom_call" | custom-call | tf_op jit(solution)/shard_map/pallas_call | solution.py:335

commit v3 on v2

--- a/solution.py
+++ b/solution.py
@@ -12,7 +12,7 @@
 BF16 = jnp.bfloat16
 F32 = jnp.float32
 
-HALO, XS, WS, WMATE, COT, AGG, ACT, PART, PAIR, GRAD, BACK, ACROSS, LAST, N_SEMS = range(14)
+HALO, XY, XX, WS, WMATE, COT, AGG, ACT, PART, PAIR, GRAD, BACK, ACROSS, LAST, N_SEMS = range(15)
 IN_X, IN_W1, IN_W2, IN_COT, IN_NB, IN_DEG, IN_ROWS, N_IN = range(8)
 
 
@@ -35,9 +35,9 @@
     sizes,
     x_hbm, w1_hbm, w2_hbm, cot_hbm, nb_hbm, deg_hbm, rows_hbm, count_ref,
     act_ref, gx_ref, gs_ref, gn_ref,
-    x_ref, w_ref, cot_ref, nb_ref, deg_ref, rows_ref,
-    chosen, edges, ids, live,
-    halo_out, halo_in, x_out, x_in, w_in, w_mate, cot_out, cot_in, agg_out, agg_in,
+    w_ref, cot_ref, nb_ref, deg_ref, rows_ref,
+    ext, chosen, edges, ids, live, inverse_ref,
+    halo_out, halo_in, x_out, x_y, x_in, w_in, w_mate, cot_out, cot_in, agg_out, agg_in,
     act_out, act_in, part_out, part_in, pair_out, pair_in, grad_out, grad_in, back_out, back_in,
     across_out, across_in, sums,
     send_sem, recv_sem, in_sem,
@@ -60,8 +60,8 @@
 
     loads = {}
     for which, src, dst in (
-        (IN_X, x_hbm, x_ref), (IN_ROWS, rows_hbm, rows_ref), (IN_W1, w1_hbm, w_ref.at[0]), (IN_W2, w2_hbm, w_ref.at[1]),
-        (IN_COT, cot_hbm, cot_ref), (IN_NB, nb_hbm, nb_ref), (IN_DEG, deg_hbm, deg_ref),
+        (IN_X, x_hbm, ext.at[:, pl.ds(0, nodes)]), (IN_ROWS, rows_hbm, rows_ref), (IN_NB, nb_hbm, nb_ref),
+        (IN_DEG, deg_hbm, deg_ref), (IN_W1, w1_hbm, w_ref.at[0]), (IN_W2, w2_hbm, w_ref.at[1]), (IN_COT, cot_hbm, cot_ref),
     ):
         loads[which] = pltpu.make_async_copy(src, dst, in_sem.at[which])
         loads[which].start()
@@ -84,18 +84,27 @@
             return carry
         lax.fori_loop(0, count, step, 0)
 
+    def from_half(i, count):
+        return 1 + lax.rem(i + max(3 * count // 8 - 1, 0), count - 1)
+
     def to_feat(body):
         def one(i):
-            other = lax.rem(me_f + 1 + i, n_feat)
+            other = lax.rem(me_f + from_half(i, n_feat), n_feat)
             body(other, other // n_x)
         each(n_feat - 1, one)
 
     def to_y(body):
         def one(i):
-            other = lax.rem(me_y + 1 + i, n_y)
+            other = lax.rem(me_y + from_half(i, n_y), n_y)
             body(other * n_x + me_x, other)
         each(n_y - 1, one)
 
+    def to_x(body):
+        def one(i):
+            other = lax.rem(me_x + 1 + i, n_x)
+            body(me_y * n_x + other, other)
+        each(n_x - 1, one)
+
     barrier = pltpu.get_barrier_semaphore()
 
     def greet(dom, feat):
@@ -103,7 +112,7 @@
 
     def to_z(body):
         def one(i):
-            other = lax.rem(me_z + 1 + i, n_z)
+            other = lax.rem(me_z + from_half(i, n_z), n_z)
             body(other * 2 + core, other)
         each(n_z - 1, one)
 
@@ -120,62 +129,91 @@
     node_id = lax.broadcasted_iota(jnp.int32, (nodes, 2 * halo), 0)
     chosen[...] = jnp.where(node_id == rows, 1.0, 0.0).astype(BF16)
     loads[IN_X].wait()
-    x = x_ref[...]
+    x = ext[:, :nodes]
     picked = dot(x, chosen[...]).astype(BF16)
     halo_out[0] = picked[:, :halo]
     halo_out[1] = picked[:, halo:]
-    loads[IN_COT].wait()
     for y in range(n_y):
         x_out[y] = x[:, y * block : (y + 1) * block]
-        cot_out[y] = cot_ref[:, y * block : (y + 1) * block]
-    x_in[me_f] = x_out[me_y]
-    cot_in[me_y] = cot_out[me_y]
-    loads[IN_W1].wait()
-    loads[IN_W2].wait()
-    w_in[me_y] = w_ref[core]
-
-    pl.semaphore_wait(barrier, n_feat - 1 + n_z - 1 + 2)
-
-    remote(halo_out.at[0], halo_in.at[1], HALO, before, me_f).start()
-    remote(halo_out.at[1], halo_in.at[0], HALO, after, me_f).start()
-    to_y(lambda f, y: remote(w_ref.at[core], w_in.at[me_y], WS, me_d, f).start())
-    to_feat(lambda f, y: remote(x_out.at[y], x_in.at[me_f], XS, me_d, f).start())
-    to_y(lambda f, y: remote(cot_out.at[y], cot_in.at[me_y], COT, me_d, f).start())
+    x_y[me_y] = x_out[me_y]
 
     loads[IN_DEG].wait()
     loads[IN_NB].wait()
     degree = deg_ref[...]
     slot = lax.broadcasted_iota(jnp.int32, (slots, nodes), 0)
     live[...] = jnp.where(slot < degree, nb_ref[...], -1)
-    ids[...] = lax.broadcasted_iota(jnp.int32, (eb, block), 0).astype(F32).astype(BF16)
+    ids[...] = lax.broadcasted_iota(jnp.int32, (eb, 2 * block), 0).astype(F32).astype(BF16)
     inverse = 1.0 / degree.astype(F32)
-
-    def count_edges(t):
-        lanes = pl.ds(pl.multiple_of((t % n_y) * block, block), block)
-        base = (t // n_y) * eb
-        mine = (live[:, lanes] - base).astype(F32).astype(BF16)
-        known = ids[...]
-        total = jnp.zeros((eb, block), BF16)
-        for k in range(slots):
-            total = total + jnp.where(known == mine[k : k + 1, :], jnp.ones((), BF16), jnp.zeros((), BF16))
-        edges[pl.ds(pl.multiple_of(base, eb), eb), lanes] = total
-
-    each((nodes + 2 * halo) // eb * n_y, count_edges)
-
-    mean = dot(x, edges[:nodes, :])
+    inverse_ref[...] = inverse
+
+    n_pairs = n_y // 2
+    pairs = [lax.rem(me_y // 2 + off, n_pairs) for off in sorted(range(n_pairs), key=lambda o: -min(o, n_pairs - o))]
+
+    def pair_lanes(pair):
+        return pl.ds(pl.multiple_of(pair * 2 * block, 2 * block), 2 * block)
+
+    def count_edges(pair):
+        lanes = pair_lanes(pair)
+
+        def one(t):
+            base = t * eb
+            mine = (live[:, lanes] - base).astype(F32).astype(BF16)
+            known = ids[...]
+            total = jnp.zeros((eb, 2 * block), BF16)
+            for k in range(slots):
+                total = total + jnp.where(known == mine[k : k + 1, :], jnp.ones((), BF16), jnp.zeros((), BF16))
+            edges[pl.ds(pl.multiple_of(base, eb), eb), lanes] = total
+
+        each((nodes + 2 * halo) // eb, one)
+
+    for pair in pairs[:-1]:
+        count_edges(pair)
+
+    loads[IN_COT].wait()
+    for y in range(n_y):
+        cot_out[y] = cot_ref[:, y * block : (y + 1) * block]
+    cot_in[me_y] = cot_out[me_y]
+    loads[IN_W1].wait()
+    loads[IN_W2].wait()
+    w_in[me_y] = w_ref[core]
+
+    pl.semaphore_wait(barrier, n_feat - 1 + n_z - 1 + 2)
+
+    remote(halo_out.at[0], halo_in.at[1], HALO, before, me_f).start()
+    remote(halo_out.at[1], halo_in.at[0], HALO, after, me_f).start()
+    to_y(lambda f, y: remote(x_out.at[y], x_y.at[me_y], XY, me_d, f).start())
+    to_y(lambda f, y: remote(w_ref.at[core], w_in.at[me_y], WS, me_d, f).start())
+    to_y(lambda f, y: remote(cot_out.at[y], cot_in.at[me_y], COT, me_d, f).start())
+
+    count_edges(pairs[-1])
     arrived(halo_in, HALO)
-    mean += dot(halo_in[0], edges[nodes : nodes + halo, :])
-    mean += dot(halo_in[1], edges[nodes + halo :, :])
-    mean = (mean * inverse).astype(BF16)
-    for y in range(n_y):
-        agg_out[y] = mean[:, y * block : (y + 1) * block]
-    to_feat(lambda f, y: remote(agg_out.at[y], agg_in.at[me_f], AGG, me_d, f).start())
+    ext[:, nodes : nodes + halo] = halo_in[0]
+    ext[:, nodes + halo :] = halo_in[1]
+    for pair in pairs:
+        lanes = pair_lanes(pair)
+        mean = (dot(ext[...], edges[:, lanes]) * inverse_ref[:, lanes]).astype(BF16)
+        agg_out[pair * 2] = mean[:, :block]
+        agg_out[pair * 2 + 1] = mean[:, block:]
+
+        def give(i):
+            y = pair * 2 + i // n_x
+            other = y * n_x + lax.rem(me_x + i, n_x)
+
+            @pl.when(other != me_f)
+            def _():
+                remote(agg_out.at[y], agg_in.at[me_f], AGG, me_d, other).start()
+
+        each(2 * n_x, give)
     agg_in[me_f] = agg_out[me_y]
+
+    arrived(x_y.at[pl.ds(0, n_y - 1)], XY)
+    to_x(lambda f, x: remote(x_y, x_in.at[:, me_x], XX, me_d, f).start())
+    x_in[:, me_x] = x_y[...]
 
     quarter = n_y * width
     arrived(w_in.at[pl.ds(0, n_y - 1)], WS)
     remote(w_in, w_mate, WMATE, mate, me_f).start()
-    arrived(x_in.at[pl.ds(0, n_feat - 1)], XS)
+    arrived(x_in.at[:, pl.ds(0, n_x - 1)], XX)
     full_x = x_in[...].reshape(wide, block)
     arrived(w_mate, WMATE)
     own_w = w_in[...].reshape(quarter, wide)
@@ -248,7 +286,8 @@
     sent(halo_out, HALO)
     sent(w_in.at[pl.ds(0, n_y - 1)], WS)
     sent(w_in, WMATE)
-    sent(x_in.at[pl.ds(0, n_feat - 1)], XS)
+    sent(x_y.at[pl.ds(0, n_y - 1)], XY)
+    sent(x_in.at[:, pl.ds(0, n_x - 1)], XX)
     sent(cot_in.at[pl.ds(0, n_y - 1)], COT)
     sent(agg_in.at[pl.ds(0, n_feat - 1)], AGG)
     sent(pair_in, PAIR)
@@ -293,19 +332,20 @@
         in_specs=[pl.BlockSpec(memory_space=pltpu.HBM)] * 7 + [pl.BlockSpec(memory_space=pltpu.SMEM)],
         out_specs=(vmem,) * 4,
         scratch_shapes=[
-            pltpu.VMEM((width, nodes), BF16),
             pltpu.VMEM((2, width, wide), BF16),
             pltpu.VMEM((width, nodes), BF16),
             pltpu.VMEM((slots, nodes), jnp.int32),
             pltpu.VMEM((1, nodes), jnp.int32),
             pltpu.VMEM((2, halo), jnp.int32),
+            pltpu.VMEM((width, nodes + 2 * halo), BF16),
             pltpu.VMEM((nodes, 2 * halo), BF16),
             pltpu.VMEM((nodes + 2 * halo, nodes), BF16),
-            pltpu.VMEM((eb, block), BF16),
+            pltpu.VMEM((eb, 2 * block), BF16),
             pltpu.VMEM((slots, nodes), jnp.int32),
+            pltpu.VMEM((1, nodes), F32),
             pltpu.VMEM((2, width, halo), BF16),
             pltpu.VMEM((2, width, halo), BF16),
-            tile(n_y), tile(n_feat),
+            tile(n_y), tile(n_y), tile(n_y, n_x),
             pltpu.VMEM((n_y, width, wide), BF16),
             pltpu.VMEM((n_y, width, wide), BF16),
             tile(n_y), tile(n_y),

time: 60.5 us -> 53.9 us (0.89)
  Pallas kernels: 59.6 us -> 53.1 us
    pallas_call x1, Pallas kernels: 58.1 us -> 51.6 us  [per_device(): pl.pallas_call(functools.partial(layer_kernel, sizes), out_shape=(jax.Sha...]
where the time goes in v3:
time: 53.9 us; the launch traced here: 53.8 us
  Pallas kernels  53.1 us (99%)
  between operations  0.64 us (1%)
    pallas_call x1, Pallas kernels, per_device(): pl.pallas_call(functools.partial(layer_kernel, sizes), out_shape=(jax.Sha...  51.6 us
    pallas_call x1, Pallas kernels, per_device(): pl.pallas_call(hand_over, out_shape=tuple((jax.ShapeDtypeStruct(a.shape,...  1.51 us

profile of v3, /device:TPU:1, one launch (start us, length us, event | category | flops | bytes accessed | tf_op | source)
XLA Modules:
  0.0 53.8 jit_solution(3094895697878663803)
XLA Ops:
  0.6 51.6 %shard_map.111 = (bf16[16,1024]{1,0:T(8,128)(2,1)}, f32[16,1024]{1,0:T(8,128)}, f32[16,512]{1,0:T(8,128)}, f32[16,512]{1,0:T(8,128)}) custom-call(bf16[16,1024]{1,0:T(8,128)(2,1)} %x_hbm.1, bf16[16,512]{1,0:T(8,128)(2,1)} %bitcast.7, bf16[16,512]{1,0:T(8,128)(2,1)} %bitcast.8, bf16[16,1024]{1,0:T(8,128)(2,1)} %cot_hbm.1, s32[16,1024]{1,0:T(8,128)} %bitcast.6, ...), custom_call_target="tpu_custom_call" | custom-call | tf_op jit(solution)/shard_map/pallas_call | solution.py:324
  52.2 1.5 %shard_map.112 = (bf16[16,1024]{1,0:T(8,128)(2,1)}, f32[16,1024]{1,0:T(8,128)}, f32[16,512]{1,0:T(8,128)}, f32[16,512]{1,0:T(8,128)}) custom-call(bf16[16,1024]{1,0:T(8,128)(2,1)} %get-tuple-element.12.refs_0_, f32[16,1024]{1,0:T(8,128)} %get-tuple-element.13.refs_1_, f32[16,512]{1,0:T(8,128)} %get-tuple-element.14.refs_2_, f32[16,512]{1,0:T(8,128)} %get-tuple-element.15.refs_3_), custom_call_target="tpu_custom_call" | custom-call | tf_op jit(solution)/shard_map/pallas_call | solution.py:375

commit v4 on v3

--- a/solution.py
+++ b/solution.py
@@ -12,7 +12,7 @@
 BF16 = jnp.bfloat16
 F32 = jnp.float32
 
-HALO, XY, XX, WS, WMATE, COT, AGG, ACT, PART, PAIR, GRAD, BACK, ACROSS, LAST, N_SEMS = range(15)
+HALO, XY, XX, WS, WMATE, COT, AGG, ACT, DIRECT, SPREAD, PAIR, BACK, LAST, GRAD, GRAD_2, ACROSS, ACROSS_2, N_SEMS = range(18)
 IN_X, IN_W1, IN_W2, IN_COT, IN_NB, IN_DEG, IN_ROWS, N_IN = range(8)
 
 
@@ -36,7 +36,7 @@
     x_hbm, w1_hbm, w2_hbm, cot_hbm, nb_hbm, deg_hbm, rows_hbm, count_ref,
     act_ref, gx_ref, gs_ref, gn_ref,
     w_ref, cot_ref, nb_ref, deg_ref, rows_ref,
-    ext, chosen, edges, ids, live, inverse_ref,
+    ext, chosen, edges, low_ref, unit_ref, inverse_ref,
     halo_out, halo_in, x_out, x_y, x_in, w_in, w_mate, cot_out, cot_in, agg_out, agg_in,
     act_out, act_in, part_out, part_in, pair_out, pair_in, grad_out, grad_in, back_out, back_in,
     across_out, across_in, sums,
@@ -47,6 +47,7 @@
     n_z = n_dom // 2
     nodes = n_y * block
     wide = w1_hbm.shape[1]
+    half_wide = wide // 2
     me_d = lax.axis_index("dom")
     me_f = lax.axis_index("feat")
     me_y = me_f // n_x
@@ -117,9 +118,9 @@
         each(n_z - 1, one)
 
     greet(far, me_f)
+    to_z(lambda d, z: greet(d, me_f))
+    to_feat(lambda f, y: greet(me_d, f))
     greet(mate, me_f)
-    to_feat(lambda f, y: greet(me_d, f))
-    to_z(lambda d, z: greet(d, me_f))
 
     slot_id = lax.broadcasted_iota(jnp.int32, (1, 2 * halo), 1)
     limit = jnp.where(slot_id < halo, count_ref[0], count_ref[1] + halo)
@@ -141,8 +142,9 @@
     loads[IN_NB].wait()
     degree = deg_ref[...]
     slot = lax.broadcasted_iota(jnp.int32, (slots, nodes), 0)
-    live[...] = jnp.where(slot < degree, nb_ref[...], -1)
-    ids[...] = lax.broadcasted_iota(jnp.int32, (eb, 2 * block), 0).astype(F32).astype(BF16)
+    nb = nb_ref[...]
+    low_ref[...] = jnp.where(slot < degree, nb % eb, -1)
+    unit_ref[...] = jnp.left_shift(jnp.ones_like(nb), 6 * (nb // eb))
     inverse = 1.0 / degree.astype(F32)
     inverse_ref[...] = inverse
 
@@ -153,20 +155,24 @@
         return pl.ds(pl.multiple_of(pair * 2 * block, 2 * block), 2 * block)
 
     def count_edges(pair):
-        lanes = pair_lanes(pair)
+        rows_once = min(128, eb)
 
         def one(t):
-            base = t * eb
-            mine = (live[:, lanes] - base).astype(F32).astype(BF16)
-            known = ids[...]
-            total = jnp.zeros((eb, 2 * block), BF16)
+            lanes = pl.ds(pl.multiple_of((pair * 2 + t % 2) * block, block), block)
+            base = (t // 2) * rows_once
+            low = low_ref[:, lanes] - base
+            unit = unit_ref[:, lanes]
+            known = lax.broadcasted_iota(jnp.int32, (rows_once, block), 0)
+            total = jnp.zeros((rows_once, block), jnp.int32)
             for k in range(slots):
-                total = total + jnp.where(known == mine[k : k + 1, :], jnp.ones((), BF16), jnp.zeros((), BF16))
-            edges[pl.ds(pl.multiple_of(base, eb), eb), lanes] = total
-
-        each((nodes + 2 * halo) // eb, one)
-
-    for pair in pairs[:-1]:
+                total = total + jnp.where(known == low[k : k + 1, :], unit[k : k + 1, :], 0)
+            for high in range((nodes + 2 * halo) // eb):
+                count = ((total >> (6 * high)) & 63).astype(F32).astype(BF16)
+                edges[pl.ds(pl.multiple_of(high * eb + base, rows_once), rows_once), lanes] = count
+
+        each(2 * eb // rows_once, one)
+
+    for pair in pairs[:2]:
         count_edges(pair)
 
     loads[IN_COT].wait()
@@ -185,7 +191,8 @@
     to_y(lambda f, y: remote(w_ref.at[core], w_in.at[me_y], WS, me_d, f).start())
     to_y(lambda f, y: remote(cot_out.at[y], cot_in.at[me_y], COT, me_d, f).start())
 
-    count_edges(pairs[-1])
+    for pair in pairs[2:]:
+        count_edges(pair)
     arrived(halo_in, HALO)
     ext[:, nodes : nodes + halo] = halo_in[0]
     ext[:, nodes + halo :] = halo_in[1]
@@ -234,42 +241,47 @@
     pair_out[1] = dot_t(grad, full_agg)
     remote(pair_out.at[1 - core], pair_in, PAIR, mate, me_f).start()
 
-    part_out[:, 0] = dot(w1_t, grad).astype(BF16).reshape(n_feat, width, block)
-    part_out[:, 1] = dot(w2_t, grad).astype(BF16).reshape(n_feat, width, block)
-    part_in[me_f] = part_out[me_f]
+    part_out[0] = dot(w1_t, grad).astype(BF16).reshape(n_feat, width, block)
+    part_out[1] = dot(w2_t, grad).astype(BF16).reshape(n_feat, width, block)
+    part_in[:, me_f] = part_out[:, me_f]
 
     arrived(pair_in, PAIR)
-    grad_out[...] = (pair_out[core] + pair_in[...]).astype(BF16).reshape(n_y, width, wide)
-    to_y(lambda f, y: remote(grad_out.at[y], grad_in.at[me_y], GRAD, me_d, f).start())
-    grad_in[me_y] = grad_out[me_y]
-    to_feat(lambda f, y: remote(part_out.at[f], part_in.at[me_f], PART, me_d, f).start())
+    for half in range(2):
+        lanes = slice(half * half_wide, (half + 1) * half_wide)
+        summed = pair_out[core, :, lanes] + pair_in[:, lanes]
+        grad_out[half] = summed.astype(BF16).reshape(n_y, width, half_wide)
+        to_y(lambda f, y: remote(grad_out.at[half, y], grad_in.at[half, me_y], GRAD + half, me_d, f).start())
+    grad_in[:, me_y] = grad_out[:, me_y]
+    to_feat(lambda f, y: remote(part_out.at[1, f], part_in.at[1, me_f], SPREAD, me_d, f).start())
+    to_feat(lambda f, y: remote(part_out.at[0, f], part_in.at[0, me_f], DIRECT, me_d, f).start())
 
     act_out[...] = (preact * s).astype(BF16).reshape(n_y, width, block)
     to_y(lambda f, y: remote(act_out.at[y], act_in.at[me_y], ACT, me_d, f).start())
     act_in[me_y] = act_out[me_y]
 
-    arrived(grad_in.at[pl.ds(0, n_y - 1)], GRAD)
-    across_out[...] = jnp.sum(grad_in[...].astype(F32), axis=0).astype(BF16)
-    to_z(lambda d, z: remote(across_out, across_in.at[me_z], ACROSS, d, me_f).start())
-    across_in[me_z] = across_out[...]
-
-    arrived(part_in.at[pl.ds(0, n_feat - 1)], PART)
-    direct, spread = [], []
-    for y in range(n_y):
-        here = part_in[pl.ds(y * n_x, n_x)].astype(F32)
-        here = jnp.sum(here, axis=0)
-        direct.append(here[0])
-        spread.append(here[1])
-    direct = jnp.concatenate(direct, axis=1)
-    spread = jnp.concatenate(spread, axis=1) * inverse
-    ext = split_dot_t(spread, edges[nodes:, :])
-    back_out[0] = ext[:, :halo]
-    back_out[1] = ext[:, halo:]
+    for half in range(2):
+        arrived(grad_in.at[half, pl.ds(0, n_y - 1)], GRAD + half)
+        across_out[half] = jnp.sum(grad_in[half].astype(F32), axis=0).astype(BF16)
+        to_z(lambda d, z: remote(across_out.at[half], across_in.at[half, me_z], ACROSS + half, d, me_f).start())
+    across_in[:, me_z] = across_out[...]
+
+    def quarters(which):
+        return jnp.concatenate(
+            [jnp.sum(part_in[which, y * n_x : (y + 1) * n_x].astype(F32), axis=0) for y in range(n_y)], axis=1
+        )
+
+    arrived(part_in.at[1, pl.ds(0, n_feat - 1)], SPREAD)
+    spread = quarters(1) * inverse
+    ends = split_dot_t(spread, edges[nodes:, :])
+    back_out[0] = ends[:, :halo]
+    back_out[1] = ends[:, halo:]
     remote(back_out.at[0], back_in.at[1], BACK, before, me_f).start()
     remote(back_out.at[1], back_in.at[0], BACK, after, me_f).start()
 
-    gx = direct + split_dot_t(spread, edges[:nodes, :])
-
+    gx = split_dot_t(spread, edges[:nodes, :])
+
+    arrived(part_in.at[0, pl.ds(0, n_feat - 1)], DIRECT)
+    gx += quarters(0)
     arrived(back_in, BACK)
     gx += split_dot_t(jnp.concatenate([back_in[0], back_in[1]], axis=1), chosen[...])
     gx_ref[...] = gx
@@ -278,8 +290,10 @@
     for y in range(n_y):
         act_ref[:, y * block : (y + 1) * block] = act_in[y]
 
-    arrived(across_in.at[pl.ds(0, n_z - 1)], ACROSS)
-    sums[core] = jnp.sum(across_in[...].astype(F32), axis=0) * (1.0 / math.sqrt(nodes * n_dom))
+    for half in range(2):
+        arrived(across_in.at[half, pl.ds(0, n_z - 1)], ACROSS + half)
+        summed = jnp.sum(across_in[half].astype(F32), axis=0) * (1.0 / math.sqrt(nodes * n_dom))
+        sums[core, :, half * half_wide : (half + 1) * half_wide] = summed
     last = remote(sums.at[core], sums.at[core], LAST, mate, me_f)
     last.start()
 
@@ -291,19 +305,24 @@
     sent(cot_in.at[pl.ds(0, n_y - 1)], COT)
     sent(agg_in.at[pl.ds(0, n_feat - 1)], AGG)
     sent(pair_in, PAIR)
-    sent(part_in.at[pl.ds(0, n_feat - 1)], PART)
-    sent(grad_in.at[pl.ds(0, n_y - 1)], GRAD)
+    sent(part_in.at[1, pl.ds(0, n_feat - 1)], SPREAD)
+    sent(part_in.at[0, pl.ds(0, n_feat - 1)], DIRECT)
     sent(act_in.at[pl.ds(0, n_y - 1)], ACT)
     sent(back_out, BACK)
-    sent(across_in.at[pl.ds(0, n_z - 1)], ACROSS)
+    for half in range(2):
+        sent(grad_in.at[half, pl.ds(0, n_y - 1)], GRAD + half)
+        sent(across_in.at[half, pl.ds(0, n_z - 1)], ACROSS + half)
     last.wait()
     gs_ref[...] = sums[0]
     gn_ref[...] = sums[1]
 
 
 def hand_over(*refs):
-    for src, dst in zip(refs[:4], refs[4:]):
-        dst[...] = src[...]
+    copies = [pltpu.make_async_copy(refs[i], refs[4 + i], refs[8].at[i]) for i in range(4)]
+    for copy in copies:
+        copy.start()
+    for copy in copies:
+        copy.wait()
 
 
 def per_device(
@@ -324,10 +343,10 @@
     act, gx, gs, gn = pl.pallas_call(
         functools.partial(layer_kernel, sizes),
         out_shape=(
-            jax.ShapeDtypeStruct((width, nodes), BF16),
-            jax.ShapeDtypeStruct((width, nodes), F32),
-            jax.ShapeDtypeStruct((width, wide), F32),
-            jax.ShapeDtypeStruct((width, wide), F32),
+            pltpu.VMEM((width, nodes), BF16),
+            pltpu.VMEM((width, nodes), F32),
+            pltpu.VMEM((width, wide), F32),
+            pltpu.VMEM((width, wide), F32),
         ),
         in_specs=[pl.BlockSpec(memory_space=pltpu.HBM)] * 7 + [pl.BlockSpec(memory_space=pltpu.SMEM)],
         out_specs=(vmem,) * 4,
@@ -340,7 +359,7 @@
             pltpu.VMEM((width, nodes + 2 * halo), BF16),
             pltpu.VMEM((nodes, 2 * halo), BF16),
             pltpu.VMEM((nodes + 2 * halo, nodes), BF16),
-            pltpu.VMEM((eb, 2 * block), BF16),
+            pltpu.VMEM((slots, nodes), jnp.int32),
             pltpu.VMEM((slots, nodes), jnp.int32),
             pltpu.VMEM((1, nodes), F32),
             pltpu.VMEM((2, width, halo), BF16),
@@ -351,22 +370,22 @@
             tile(n_y), tile(n_y),
             tile(n_y), tile(n_feat),
             tile(n_y), tile(n_y),
-            tile(n_feat, 2), tile(n_feat, 2),
+            tile(2, n_feat), tile(2, n_feat),
             pltpu.VMEM((2, n_y * width, wide), F32),
             pltpu.VMEM((n_y * width, wide), F32),
-            pltpu.VMEM((n_y, width, wide), BF16),
-            pltpu.VMEM((n_y, width, wide), BF16),
+            pltpu.VMEM((2, n_y, width, wide // 2), BF16),
+            pltpu.VMEM((2, n_y, width, wide // 2), BF16),
             pltpu.VMEM((2, width, halo), F32),
             pltpu.VMEM((2, width, halo), F32),
-            pltpu.VMEM((width, wide), BF16),
-            pltpu.VMEM((n_dom // 2, width, wide), BF16),
+            pltpu.VMEM((2, width, wide // 2), BF16),
+            pltpu.VMEM((2, n_dom // 2, width, wide // 2), BF16),
             pltpu.VMEM((2, width, wide), F32),
             pltpu.SemaphoreType.DMA((N_SEMS,)),
             pltpu.SemaphoreType.DMA((N_SEMS,)),
             pltpu.SemaphoreType.DMA((N_IN,)),
         ],
         compiler_params=pltpu.CompilerParams(
-            collective_id=0, has_side_effects=True, vmem_limit_bytes=64 * 1024 * 1024
+            collective_id=0, has_side_effects=True, vmem_limit_bytes=(64 * 1024 - 256) * 1024
         ),
     )(
         features, self_weight.T, neigh_weight.T, cotangent, neighbours.T, degrees.reshape(1, nodes),
@@ -376,8 +395,9 @@
         hand_over,
         out_shape=tuple(jax.ShapeDtypeStruct(a.shape, a.dtype) for a in (act, gx, gs, gn)),
         in_specs=[vmem] * 4,
-        out_specs=(vmem,) * 4,
-    )(act, gx, gs, gn)
+        out_specs=(pl.BlockSpec(memory_space=pltpu.HBM),) * 4,
+        scratch_shapes=[pltpu.SemaphoreType.DMA((4,))],
+    )(*(pltpu.with_memory_space_constraint(a, pltpu.VMEM) for a in (act, gx, gs, gn)))
     return act, gx, gs.T, gn.T
 
 

time: 53.9 us -> 50.4 us (0.935)
  Pallas kernels: 53.1 us -> 49.6 us
    pallas_call x1, Pallas kernels: 51.6 us -> 48.9 us  [per_device(): pl.pallas_call(functools.partial(layer_kernel, sizes), out_shape=(pltpu.V...]
    pallas_call x1, Pallas kernels: 1.51 us -> 0.7 us  [per_device(): pl.pallas_call(hand_over, out_shape=tuple((jax.ShapeDtypeStruct(a.shape,...]
where the time goes in v4:
time: 50.4 us; the launch traced here: 50.3 us
  Pallas kernels  49.6 us (98%)
  between operations  0.64 us (1%)
    pallas_call x1, Pallas kernels, per_device(): pl.pallas_call(functools.partial(layer_kernel, sizes), out_shape=(pltpu.V...  48.9 us

profile of v4, /device:TPU:1, one launch (start us, length us, event | category | flops | bytes accessed | tf_op | source)
XLA Modules:
  0.0 50.3 jit_solution(7647401441495463586)
XLA Ops:
  0.6 48.9 %shard_map.111 = (bf16[16,1024]{1,0:T(8,128)(2,1)S(1)}, f32[16,1024]{1,0:T(8,128)S(1)}, f32[16,512]{1,0:T(8,128)S(1)}, f32[16,512]{1,0:T(8,128)S(1)}) custom-call(bf16[16,1024]{1,0:T(8,128)(2,1)} %x_hbm.1, bf16[16,512]{1,0:T(8,128)(2,1)} %bitcast.7, bf16[16,512]{1,0:T(8,128)(2,1)} %bitcast.8, bf16[16,1024]{1,0:T(8,128)(2,1)} %cot_hbm.1, s32[16,1024]{1,0:T(8,128)} %bitcast.6, ...), custom_call_target="tpu_custom_call" | custom-call | tf_op jit(solution)/shard_map/pallas_call | solution.py:343
  49.6 0.7 %shard_map.112 = (bf16[16,1024]{1,0:T(8,128)(2,1)}, f32[16,1024]{1,0:T(8,128)}, f32[16,512]{1,0:T(8,128)}, f32[16,512]{1,0:T(8,128)}) custom-call(bf16[16,1024]{1,0:T(8,128)(2,1)S(1)} %get-tuple-element.12.refs_0_, f32[16,1024]{1,0:T(8,128)S(1)} %get-tuple-element.13.refs_1_, f32[16,512]{1,0:T(8,128)S(1)} %get-tuple-element.14.refs_2_, ...), custom_call_target="tpu_custom_call" | custom-call | tf_op jit(solution)/shard_map/pallas_call | solution.py:394

commit v5 on v4

v5 whole, which is shorter than its diff:
```python
import functools
import math

import jax
import jax.numpy as jnp
from jax import lax
from jax.experimental import pallas as pl
from jax.experimental.pallas import tpu as pltpu
from jax.sharding import PartitionSpec as P

MESH = pl.DeviceIdType.MESH
BF16 = jnp.bfloat16
F32 = jnp.float32

HALO, XS, WS, WMATE, COT, AGG, ACT, DIRECT, SPREAD, PAIR, BACK, LAST, LAST_2, GRAD, GRAD_2, ACROSS, ACROSS_2, N_SEMS = range(18)
IN_X, IN_W1, IN_W2, IN_COT, IN_NB, IN_DEG, IN_ROWS, IN_COUNT, N_IN = range(9)


def dot(a, b):
    return jnp.dot(a, b, preferred_element_type=F32)


def dot_t(a, b):
    return lax.dot_general(a, b, (((1,), (1,)), ((), ())), preferred_element_type=F32)


def split_dot_t(a, b):
    high = a.astype(BF16)
    low = (a - high.astype(F32)).astype(BF16)
    both = dot_t(jnp.concatenate([high, low], axis=0), b)
    return both[: a.shape[0]] + both[a.shape[0] :]


def layer_kernel(
    sizes,
    x_hbm, w1_hbm, w2_hbm, cot_hbm, nb_hbm, deg_hbm, rows_hbm, count_hbm,
    act_ref, gx_ref, gs_ref, gn_ref,
    w_ref, cot_ref, nb_ref, deg_ref, rows_ref, count_ref,
    ext, chosen, edges, low_ref, unit_ref, inverse_ref,
    halo_out, halo_in, x_out, x_in, w_in, w_mate, cot_out, cot_in, agg_out, agg_in,
    act_out, act_in, part_out, part_in, pair_out, pair_in, grad_out, grad_in, back_out, back_in,
    across_out, across_in, sums,
    send_sem, recv_sem, in_sem,
):
    n_dom, n_feat, n_b, width, block, halo, slots, eb = sizes
    n_q = n_feat // n_b
    n_z = n_dom // 2
    nodes = n_b * block
    wide = w1_hbm.shape[1]
    half_wide = wide // 2
    me_d = lax.axis_index("dom")
    me_f = lax.axis_index("feat")
    me_b = me_f % n_b
    me_q = me_f // n_b
    me_z = me_d // 2
    core = me_d % 2
    mate = me_d + 1 - 2 * core
    before = lax.rem(me_d + n_dom - 1, n_dom)
    after = lax.rem(me_d + 1, n_dom)
    far = jnp.where(core == 0, before, after)

    loads = {}
    for which, src, dst in (
        (IN_X, x_hbm, ext.at[:, pl.ds(0, nodes)]), (IN_ROWS, rows_hbm, rows_ref), (IN_COUNT, count_hbm, count_ref),
        (IN_NB, nb_hbm, nb_ref),
        (IN_DEG, deg_hbm, deg_ref), (IN_W1, w1_hbm, w_ref.at[0]), (IN_W2, w2_hbm, w_ref.at[1]), (IN_COT, cot_hbm, cot_ref),
    ):
        loads[which] = pltpu.make_async_copy(src, dst, in_sem.at[which])
        loads[which].start()

    def remote(src, dst, which, dom, feat):
        return pltpu.make_async_remote_copy(
            src_ref=src, dst_ref=dst, send_sem=send_sem.at[which], recv_sem=recv_sem.at[which],
            device_id={"dom": dom, "feat": feat}, device_id_type=MESH,
        )

    def arrived(ref, which):
        remote(ref, ref, which, me_d, me_f).wait_recv()

    def sent(ref, which):
        remote(ref, ref, which, me_d, me_f).wait_send()

    def each(count, body):
        def step(i, carry):
            body(i)
            return carry
        lax.fori_loop(0, count, step, 0)

    def from_half(i, count):
        return 1 + lax.rem(i + max(3 * count // 8 - 1, 0), count - 1)

    def to_feat(body):
        def one(i):
            other = lax.rem(me_f + from_half(i, n_feat), n_feat)
            body(other, lax.rem(other, n_b))
        each(n_feat - 1, one)

    def to_group(body):
        def one(i):
            other = lax.rem(me_b + from_half(i, n_b), n_b)
            body(me_q * n_b + other, other)
        each(n_b - 1, one)

    barrier = pltpu.get_barrier_semaphore()

    def greet(dom, feat):
        pl.semaphore_signal(barrier, inc=1, device_id={"dom": dom, "feat": feat}, device_id_type=MESH)

    def to_z(body):
        def one(i):
            other = lax.rem(me_z + from_half(i, n_z), n_z)
            body(other * 2 + core, other)
        each(n_z - 1, one)

    greet(far, me_f)
    to_z(lambda d, z: greet(d, me_f))
    to_feat(lambda f, b: greet(me_d, f))
    greet(mate, me_f)

    slot_id = lax.broadcasted_iota(jnp.int32, (1, 2 * halo), 1)
    loads[IN_COUNT].wait()
    limit = jnp.where(slot_id < halo, count_ref[0], count_ref[1] + halo)
    loads[IN_ROWS].wait()
    rows = jnp.concatenate([rows_ref[0:1, :], rows_ref[1:2, :]], axis=1)
    rows = jnp.where(slot_id < limit, rows, -1)
    node_id = lax.broadcasted_iota(jnp.int32, (nodes, 2 * halo), 0)
    chosen[...] = jnp.where(node_id == rows, 1.0, 0.0).astype(BF16)
    loads[IN_X].wait()
    x = ext[:, :nodes]
    picked = dot(x, chosen[...]).astype(BF16)
    halo_out[0] = picked[:, :halo]
    halo_out[1] = picked[:, halo:]
    for b in range(n_b):
        x_out[b] = x[:, b * block : (b + 1) * block]
    x_in[me_f] = x_out[me_b]

    loads[IN_DEG].wait()
    loads[IN_NB].wait()
    degree = deg_ref[...]
    slot = lax.broadcasted_iota(jnp.int32, (slots, nodes), 0)
    nb = nb_ref[...]
    low_ref[...] = jnp.where(slot < degree, nb % eb, -1)
    unit_ref[...] = jnp.left_shift(jnp.ones_like(nb), 6 * (nb // eb))
    inverse = 1.0 / degree.astype(F32)
    inverse_ref[...] = inverse

    n_pairs = n_b // 2
    pairs = [lax.rem(me_b // 2 + off, n_pairs) for off in sorted(range(n_pairs), key=lambda o: -min(o, n_pairs - o))]

    def pair_lanes(pair):
        return pl.ds(pl.multiple_of(pair * 2 * block, 2 * block), 2 * block)

    def count_edges(pair):
        rows_once = min(128, eb)

        def one(t):
            lanes = pl.ds(pl.multiple_of((pair * 2 + t % 2) * block, block), block)
            base = (t // 2) * rows_once
            low = low_ref[:, lanes] - base
            unit = unit_ref[:, lanes]
            known = lax.broadcasted_iota(jnp.int32, (rows_once, block), 0)
            total = jnp.zeros((rows_once, block), jnp.int32)
            for k in range(slots):
                total = total + jnp.where(known == low[k : k + 1, :], unit[k : k + 1, :], 0)
            for high in range((nodes + 2 * halo) // eb):
                count = ((total >> (6 * high)) & 63).astype(F32).astype(BF16)
                edges[pl.ds(pl.multiple_of(high * eb + base, rows_once), rows_once), lanes] = count

        each(2 * eb // rows_once, one)

    for pair in pairs[:2]:
        count_edges(pair)

    loads[IN_COT].wait()
    for b in range(n_b):
        cot_out[b] = cot_ref[:, b * block : (b + 1) * block]
    cot_in[me_b] = cot_out[me_b]
    loads[IN_W1].wait()
    loads[IN_W2].wait()
    w_in[me_b] = w_ref[core]

    pl.semaphore_wait(barrier, n_feat - 1 + n_z - 1 + 2)

    remote(halo_out.at[0], halo_in.at[1], HALO, before, me_f).start()
    remote(halo_out.at[1], halo_in.at[0], HALO, after, me_f).start()
    to_group(lambda f, b: remote(w_ref.at[core], w_in.at[me_b], WS, me_d, f).start())
    to_group(lambda f, b: remote(cot_out.at[b], cot_in.at[me_b], COT, me_d, f).start())
    to_feat(lambda f, b: remote(x_out.at[b], x_in.at[me_f], XS, me_d, f).start())

    for pair in pairs[2:]:
        count_edges(pair)
    arrived(halo_in, HALO)
    ext[:, nodes : nodes + halo] = halo_in[0]
    ext[:, nodes + halo :] = halo_in[1]
    for pair in pairs:
        lanes = pair_lanes(pair)
        mean = (dot(ext[...], edges[:, lanes]) * inverse_ref[:, lanes]).astype(BF16)
        agg_out[pair * 2] = mean[:, :block]
        agg_out[pair * 2 + 1] = mean[:, block:]

        def give(i):
            b = pair * 2 + i // n_q
            other = lax.rem(me_q + i + n_q // 2, n_q) * n_b + b

            @pl.when(other != me_f)
            def _():
                remote(agg_out.at[b], agg_in.at[me_f], AGG, me_d, other).start()

        each(2 * n_q, give)
    agg_in[me_f] = agg_out[me_b]

    quarter = n_b * width
    arrived(w_in.at[pl.ds(0, n_b - 1)], WS)
    remote(w_in, w_mate, WMATE, mate, me_f).start()
    arrived(x_in.at[pl.ds(0, n_feat - 1)], XS)
    full_x = x_in[...].reshape(wide, block)
    arrived(w_mate, WMATE)
    own_w = w_in[...].reshape(quarter, wide)
    other_w = w_mate[...].reshape(quarter, wide)
    w1 = jnp.where(core == 0, own_w, other_w)
    w2 = jnp.where(core == 0, other_w, own_w)
    preact = dot(w1, full_x)
    arrived(cot_in.at[pl.ds(0, n_b - 1)], COT)
    cot = cot_in[...].reshape(quarter, block).astype(F32)
    arrived(agg_in.at[pl.ds(0, n_feat - 1)], AGG)
    full_agg = agg_in[...].reshape(wide, block)
    preact += dot(w2, full_agg)
    s = jax.nn.sigmoid(preact)
    grad = (cot * s * (1.0 + preact * (1.0 - s))).astype(BF16)
    pair_out[...] = dot_t(grad, jnp.where(core == 0, full_agg, full_x))
    remote(pair_out, pair_in, PAIR, mate, me_f).start()
    weight_grad = dot_t(grad, jnp.where(core == 0, full_x, full_agg))

    w1_t = w1.T
    w2_t = w2.T
    part_out[0] = dot(w1_t, grad).astype(BF16).reshape(n_feat, width, block)
    part_out[1] = dot(w2_t, grad).astype(BF16).reshape(n_feat, width, block)
    part_in[:, me_f] = part_out[:, me_f]

    arrived(pair_in, PAIR)
    for half in range(2):
        lanes = slice(half * half_wide, (half + 1) * half_wide)
        summed = weight_grad[:, lanes] + pair_in[:, lanes]
        grad_out[half] = summed.astype(BF16).reshape(n_b, width, half_wide)
        to_group(lambda f, b: remote(grad_out.at[half, b], grad_in.at[half, me_b], GRAD + half, me_d, f).start())
    grad_in[:, me_b] = grad_out[:, me_b]
    to_feat(lambda f, b: remote(part_out.at[1, f], part_in.at[1, me_f], SPREAD, me_d, f).start())
    to_feat(lambda f, b: remote(part_out.at[0, f], part_in.at[0, me_f], DIRECT, me_d, f).start())

    act_out[...] = (preact * s).astype(BF16).reshape(n_b, width, block)
    to_group(lambda f, b: remote(act_out.at[b], act_in.at[me_b], ACT, me_d, f).start())
    act_in[me_b] = act_out[me_b]

    for half in range(2):
        arrived(grad_in.at[half, pl.ds(0, n_b - 1)], GRAD + half)
        across_out[half] = jnp.sum(grad_in[half].astype(F32), axis=0).astype(BF16)
        to_z(lambda d, z: remote(across_out.at[half], across_in.at[half, me_z], ACROSS + half, d, me_f).start())
    across_in[:, me_z] = across_out[...]

    def quarters(which):
        total = jnp.sum(part_in[which].reshape(n_q, n_b, width, block).astype(F32), axis=0)
        return jnp.concatenate([total[b] for b in range(n_b)], axis=1)

    arrived(part_in.at[1, pl.ds(0, n_feat - 1)], SPREAD)
    spread = quarters(1) * inverse
    ends = split_dot_t(spread, edges[nodes:, :])
    back_out[0] = ends[:, :halo]
    back_out[1] = ends[:, halo:]
    remote(back_out.at[0], back_in.at[1], BACK, before, me_f).start()
    remote(back_out.at[1], back_in.at[0], BACK, after, me_f).start()

    gx = split_dot_t(spread, edges[:nodes, :])

    arrived(part_in.at[0, pl.ds(0, n_feat - 1)], DIRECT)
    gx += quarters(0)
    arrived(back_in, BACK)
    gx += split_dot_t(jnp.concatenate([back_in[0], back_in[1]], axis=1), chosen[...])
    gx_ref[...] = gx

    arrived(act_in.at[pl.ds(0, n_b - 1)], ACT)
    for b in range(n_b):
        act_ref[:, b * block : (b + 1) * block] = act_in[b]

    lasts = []
    for half in range(2):
        arrived(across_in.at[half, pl.ds(0, n_z - 1)], ACROSS + half)
        summed = jnp.sum(across_in[half].astype(F32), axis=0) * (1.0 / math.sqrt(nodes * n_dom))
        sums[core, half] = summed
        lasts.append(remote(sums.at[core, half], sums.at[core, half], LAST + half, mate, me_f))
        lasts[half].start()

    sent(halo_out, HALO)
    sent(w_in.at[pl.ds(0, n_b - 1)], WS)
    sent(w_in, WMATE)
    sent(x_in.at[pl.ds(0, n_feat - 1)], XS)
    sent(cot_in.at[pl.ds(0, n_b - 1)], COT)
    sent(agg_in.at[pl.ds(0, n_feat - 1)], AGG)
    sent(pair_in, PAIR)
    sent(part_in.at[1, pl.ds(0, n_feat - 1)], SPREAD)
    sent(part_in.at[0, pl.ds(0, n_feat - 1)], DIRECT)
    sent(act_in.at[pl.ds(0, n_b - 1)], ACT)
    sent(back_out, BACK)
    for half in range(2):
        sent(grad_in.at[half, pl.ds(0, n_b - 1)], GRAD + half)
        sent(across_in.at[half, pl.ds(0, n_z - 1)], ACROSS + half)
    for half in range(2):
        lanes = slice(half * half_wide, (half + 1) * half_wide)
        lasts[half].wait()
        gs_ref[:, lanes] = sums[0, half]
        gn_ref[:, lanes] = sums[1, half]


def hand_over(*refs):
    copies = [pltpu.make_async_copy(refs[i], refs[4 + i], refs[8].at[i]) for i in range(4)]
    for copy in copies:
        copy.start()
    for copy in copies:
        copy.wait()


def per_device(
    features, self_weight, neigh_weight, cotangent, neighbours, degrees, send_rows, send_count
):
    width, nodes = features.shape
    wide = self_weight.shape[0]
    slots = neighbours.shape[1]
    halo = send_rows.shape[1]
    n_dom = lax.axis_size("dom")
    n_feat = lax.axis_size("feat")
    block = 128
    n_b = nodes // block
    eb = min(256, 2 * halo)
    sizes = (n_dom, n_feat, n_b, width, block, halo, slots, eb)
    vmem = pl.BlockSpec(memory_space=pltpu.VMEM)
    tile = lambda *lead: pltpu.VMEM((*lead, width, block), BF16)
    act, gx, gs, gn = pl.pallas_call(
        functools.partial(layer_kernel, sizes),
        out_shape=(
            pltpu.VMEM((width, nodes), BF16),
            pltpu.VMEM((width, nodes), F32),
            pltpu.VMEM((width, wide), F32),
            pltpu.VMEM((width, wide), F32),
        ),
        in_specs=[pl.BlockSpec(memory_space=pltpu.HBM)] * 8,
        out_specs=(vmem,) * 4,
        scratch_shapes=[
            pltpu.VMEM((2, width, wide), BF16),
            pltpu.VMEM((width, nodes), BF16),
            pltpu.VMEM((slots, nodes), jnp.int32),
            pltpu.VMEM((1, nodes), jnp.int32),
            pltpu.VMEM((2, halo), jnp.int32),
            pltpu.SMEM((2,), jnp.int32),
            pltpu.VMEM((width, nodes + 2 * halo), BF16),
            pltpu.VMEM((nodes, 2 * halo), BF16),
            pltpu.VMEM((nodes + 2 * halo, nodes), BF16),
            pltpu.VMEM((slots, nodes), jnp.int32),
            pltpu.VMEM((slots, nodes), jnp.int32),
            pltpu.VMEM((1, nodes), F32),
            pltpu.VMEM((2, width, halo), BF16),
            pltpu.VMEM((2, width, halo), BF16),
            tile(n_b), tile(n_feat),
            pltpu.VMEM((n_b, width, wide), BF16),
            pltpu.VMEM((n_b, width, wide), BF16),
            tile(n_b), tile(n_b),
            tile(n_b), tile(n_feat),
            tile(n_b), tile(n_b),
            tile(2, n_feat), tile(2, n_feat),
            pltpu.VMEM((n_b * width, wide), F32),
            pltpu.VMEM((n_b * width, wide), F32),
            pltpu.VMEM((2, n_b, width, wide // 2), BF16),
            pltpu.VMEM((2, n_b, width, wide // 2), BF16),
            pltpu.VMEM((2, width, halo), F32),
            pltpu.VMEM((2, width, halo), F32),
            pltpu.VMEM((2, width, wide // 2), BF16),
            pltpu.VMEM((2, n_dom // 2, width, wide // 2), BF16),
            pltpu.VMEM((2, 2, width, wide // 2), F32),
            pltpu.SemaphoreType.DMA((N_SEMS,)),
            pltpu.SemaphoreType.DMA((N_SEMS,)),
            pltpu.SemaphoreType.DMA((N_IN,)),
        ],
        compiler_params=pltpu.CompilerParams(
            collective_id=0, has_side_effects=True, vmem_limit_bytes=(64 * 1024 - 256) * 1024
        ),
    )(
        features, self_weight.T, neigh_weight.T, cotangent, neighbours.T, degrees.reshape(1, nodes),
        send_rows, send_count,
    )
    act, gx, gs, gn = pl.pallas_call(
        hand_over,
        out_shape=tuple(jax.ShapeDtypeStruct(a.shape, a.dtype) for a in (act, gx, gs, gn)),
        in_specs=[vmem] * 4,
        out_specs=(pl.BlockSpec(memory_space=pltpu.HBM),) * 4,
        scratch_shapes=[pltpu.SemaphoreType.DMA((4,))],
    )(*(pltpu.with_memory_space_constraint(a, pltpu.VMEM) for a in (act, gx, gs, gn)))
    return act, gx, gs.T, gn.T


def solution(mesh):
    return jax.shard_map(
        per_device,
        mesh=mesh,
        in_specs=(
            P("feat", "dom"),
            P(None, "feat"),
            P(None, "feat"),
            P("feat", "dom"),
            P("dom", None),
            P("dom"),
            P("dom", None),
            P("dom"),
        ),
        out_specs=(P("feat", "dom"), P("feat", "dom"), P(None, "feat"), P(None, "feat")),
        check_vma=False,
    )
```

time: 50.4 us -> 49.6 us (0.984)
  Pallas kernels: 49.6 us -> 48.8 us
    pallas_call x1, Pallas kernels: 48.9 us -> 48.1 us  [per_device(): pl.pallas_call(functools.partial(layer_kernel, sizes), out_shape=(pltpu.V...]
where the time goes in v5:
time: 49.6 us; the launch traced here: 49.5 us
  Pallas kernels  48.8 us (98%)
  between operations  0.64 us (1%)
    pallas_call x1, Pallas kernels, per_device(): pl.pallas_call(functools.partial(layer_kernel, sizes), out_shape=(pltpu.V...  48.1 us

profile of v5, /device:TPU:1, one launch (start us, length us, event | category | flops | bytes accessed | tf_op | source)
XLA Modules:
  0.0 49.5 jit_solution(8711109862695675361)
XLA Ops:
  0.6 48.1 %shard_map.111 = (bf16[16,1024]{1,0:T(8,128)(2,1)S(1)}, f32[16,1024]{1,0:T(8,128)S(1)}, f32[16,512]{1,0:T(8,128)S(1)}, f32[16,512]{1,0:T(8,128)S(1)}) custom-call(bf16[16,1024]{1,0:T(8,128)(2,1)} %x_hbm.1, bf16[16,512]{1,0:T(8,128)(2,1)} %bitcast.7, bf16[16,512]{1,0:T(8,128)(2,1)} %bitcast.8, bf16[16,1024]{1,0:T(8,128)(2,1)} %cot_hbm.1, s32[16,1024]{1,0:T(8,128)} %bitcast.6, ...), custom_call_target="tpu_custom_call" | custom-call | tf_op jit(solution)/shard_map/pallas_call | solution.py:336
  48.8 0.7 %shard_map.112 = (bf16[16,1024]{1,0:T(8,128)(2,1)}, f32[16,1024]{1,0:T(8,128)}, f32[16,512]{1,0:T(8,128)}, f32[16,512]{1,0:T(8,128)}) custom-call(bf16[16,1024]{1,0:T(8,128)(2,1)S(1)} %get-tuple-element.12.refs_0_, f32[16,1024]{1,0:T(8,128)S(1)} %get-tuple-element.13.refs_1_, f32[16,512]{1,0:T(8,128)S(1)} %get-tuple-element.14.refs_2_, ...), custom_call_target="tpu_custom_call" | custom-call | tf_op jit(solution)/shard_map/pallas_call | solution.py:388

commit v6 on v5

--- a/solution.py
+++ b/solution.py
@@ -87,7 +87,7 @@
         lax.fori_loop(0, count, step, 0)
 
     def from_half(i, count):
-        return 1 + lax.rem(i + max(3 * count // 8 - 1, 0), count - 1)
+        return count // 2 + (1 - 2 * (i % 2)) * ((i + 1) // 2)
 
     def to_feat(body):
         def one(i):

time: 49.6 us -> 49.4 us (level)
  no operation moved by 1% of the time
where the time goes in v6:
time: 49.4 us; the launch traced here: 49.2 us
  Pallas kernels  48.6 us (98%)
  between operations  0.64 us (1%)
    pallas_call x1, Pallas kernels, per_device(): pl.pallas_call(functools.partial(layer_kernel, sizes), out_shape=(pltpu.V...  47.9 us

profile of v6, /device:TPU:1, one launch (start us, length us, event | category | flops | bytes accessed | tf_op | source)
XLA Modules:
  0.0 49.2 jit_solution(11846457796322937586)
XLA Ops:
  0.6 47.9 %shard_map.111 = (bf16[16,1024]{1,0:T(8,128)(2,1)S(1)}, f32[16,1024]{1,0:T(8,128)S(1)}, f32[16,512]{1,0:T(8,128)S(1)}, f32[16,512]{1,0:T(8,128)S(1)}) custom-call(bf16[16,1024]{1,0:T(8,128)(2,1)} %x_hbm.1, bf16[16,512]{1,0:T(8,128)(2,1)} %bitcast.7, bf16[16,512]{1,0:T(8,128)(2,1)} %bitcast.8, bf16[16,1024]{1,0:T(8,128)(2,1)} %cot_hbm.1, s32[16,1024]{1,0:T(8,128)} %bitcast.6, ...), custom_call_target="tpu_custom_call" | custom-call | tf_op jit(solution)/shard_map/pallas_call | solution.py:336
  48.5 0.7 %shard_map.112 = (bf16[16,1024]{1,0:T(8,128)(2,1)}, f32[16,1024]{1,0:T(8,128)}, f32[16,512]{1,0:T(8,128)}, f32[16,512]{1,0:T(8,128)}) custom-call(bf16[16,1024]{1,0:T(8,128)(2,1)S(1)} %get-tuple-element.12.refs_0_, f32[16,1024]{1,0:T(8,128)S(1)} %get-tuple-element.13.refs_1_, f32[16,512]{1,0:T(8,128)S(1)} %get-tuple-element.14.refs_2_, ...), custom_call_target="tpu_custom_call" | custom-call | tf_op jit(solution)/shard_map/pallas_call | solution.py:388
